TPU v7x, 32 devices: a whole 2x2x4 slice. The times are simulated.
32 devices in a mesh: sec: 4 (over y, x), lat: 4 (over z), col: 2 (over core).
Axes of the slice: x: 2, y: 2, z: 4, core: 2. Of those that a mesh axis runs over, the one named last changes fastest.
Arguments:
- physical_state: bfloat16 [32, 64, 5120], P(('sec', 'lat', 'col')), may hold values from -6 to 6
- parallel_lengths: int32 [32], P(('sec', 'lat', 'col')), may hold values from 20 to 5120, as said below
- zonal_mode_assignment: int32 [856], replicated, may hold values from 0 to 640, as said below
- weighted_associated_polynomials: bfloat16 [856, 640, 32], P('lat', None, ('sec', 'col')), may hold values from -1 to 1
- marine_tracer_state: float32 [8, 128, 4096], P(None, ('sec', 'lat', 'col')), may hold values from -6 to 6
- lateral_diffusivity: float32 [128, 4096], P(('sec', 'lat', 'col')), may hold values from 0.015 to 0.15
- depthwise_diffusivity: float32 [128, 4096], P(('sec', 'lat', 'col')), may hold values from 0.02 to 0.2
- water_indicator: int32 [128, 4096], P(('sec', 'lat', 'col')), may hold values 0 or 1
- overlying_parallel: int32 [128], P(('sec', 'lat', 'col')), may hold values from 0 to 31, as said below
- underlying_marine_parallel: int32 [32], P(('sec', 'lat', 'col')), may hold values from 0 to 127, as said below
Outputs:
- harmonic_amounts: float32 [640, 856, 128], P(('sec', 'col'), 'lat')
- ocean_next: float32 [8, 128, 4096], P(None, ('sec', 'lat', 'col'))
Inputs may be any that keep to these rules, and one draw needn't show every extreme that they name: `parallel_lengths`: row j holds 20 + 4 * min(max(b + s * j, 0), 1275) points, with s = 42 and one offset b from (5100) // 4 - s * (31) to 0; the first row holds 20 points and the last 5120. `zonal_mode_assignment`: every wavenumber below 640 sits in exactly one slot; the other slots hold 640, meaning empty; slots s with equal s // 214 form a block, at least one block has all its slots taken. overlying_parallel[r] lies between (r // 4 - 1) * 1 and (r // 4 + 2) - 1; some rows reach the lower end and some the upper end. underlying_marine_parallel[j] lies between (j - 1) * 4 and (j + 2) * 4 - 1; some rows reach the lower end and some the upper end.
All inputs are finite; a program needn't handle non-finite values. No bound on the sum of `water_indicator` on one device may be relied on, other than what follows from the above.
Results may differ from a plain program's by a relative error of at most 0.004.
Values may be sent and summed in bfloat16 or wider, within the bound.
A program may use at most 256 MiB of HBM per device.

v0:
```python
import functools

import jax
import jax.numpy as jnp
from jax import lax
from jax.experimental import pallas as pl
from jax.experimental.pallas import tpu as pltpu
from jax.sharding import PartitionSpec as P

OSTEPS = 4
LOW = 8
CHUNK = 256
SLOT_PAD = 16

two_pi = 6.283185307179586
thermal_transfer_factor = 0.8
force_coef = 0.1

GROUP = ("sec", "col")
LINE = ("sec", "lat", "col")


def angle_tables(points, wave_count, grid_width):
    low = jnp.arange(LOW, dtype=jnp.float32)
    mid = jnp.arange(CHUNK // LOW, dtype=jnp.float32) * LOW
    high = jnp.arange(grid_width // CHUNK, dtype=jnp.float32) * CHUNK
    place = jnp.concatenate([low, mid, high])
    count = points.astype(jnp.float32)
    product = place[:, None] * jnp.arange(wave_count, dtype=jnp.float32)[None, :]
    residue = product - jnp.round(product / count) * count
    angle = residue * (jnp.float32(two_pi) / count)
    scale = jnp.where(jnp.arange(place.shape[0]) >= LOW + CHUNK // LOW, 1.0 / jnp.sqrt(count), 1.0)
    return jnp.stack([jnp.cos(angle), -jnp.sin(angle)]) * scale[None, :, None]


MESH = pl.DeviceIdType.MESH


def place_of(index, lat_count, col_count):
    return {
        "sec": index // (lat_count * col_count),
        "lat": index // col_count % lat_count,
        "col": index % col_count,
    }


def exchange_kernel(
    sizes,
    points_ref,
    table_ref,
    slots_ref,
    x_ref,
    weight_ref,
    *refs,
):
    sec_count, lat_count, col_count = sizes
    halo, coef_out, weight_out, before, after = refs[:5]
    (base_ref, acc_ref, mine_ref, local_sem, weight_send, weight_recv, halo_send, halo_recv,
     lat_send, lat_recv, sec_send, sec_recv, col_send, col_recv) = refs[5:]
    groups = sec_count * col_count
    devices = groups * lat_count
    sec, lat, col = (lax.axis_index(name) for name in LINE)
    group = sec * col_count + col
    line = (sec * lat_count + lat) * col_count + col
    following = place_of((line + 1) % devices, lat_count, col_count)
    previous = place_of((line + devices - 1) % devices, lat_count, col_count)

    def group_place(step):
        other = (group + step) % groups
        return other, {"sec": other // col_count, "lat": lat, "col": other % col_count}

    def lat_place(step):
        other = (lat + step) % lat_count
        return other, {"sec": sec, "lat": other, "col": col}

    barrier = pltpu.get_barrier_semaphore()
    for place in (following, previous):
        pl.semaphore_signal(barrier, inc=1, device_id=place, device_id_type=MESH)

    @pl.loop(1, groups)
    def _(step):
        pl.semaphore_signal(barrier, inc=1, device_id=group_place(step)[1], device_id_type=MESH)

    @pl.loop(1, lat_count)
    def _(step):
        pl.semaphore_signal(barrier, inc=1, device_id=lat_place(step)[1], device_id_type=MESH)

    pl.semaphore_wait(barrier, groups + lat_count)

    def weight_copy(step):
        other, place = group_place(step)
        return pltpu.make_async_remote_copy(
            src_ref=weight_ref.at[other],
            dst_ref=weight_out.at[group],
            send_sem=weight_send.at[step],
            recv_sem=weight_recv.at[step],
            device_id=place,
            device_id_type=MESH,
        )

    def halo_copy(side):
        return pltpu.make_async_remote_copy(
            src_ref=halo,
            dst_ref=(before, after)[side],
            send_sem=halo_send.at[side],
            recv_sem=halo_recv.at[side],
            device_id=(following, previous)[side],
            device_id_type=MESH,
        )

    has_next, has_previous = line < devices - 1, line > 0

    def lat_copy(step):
        other, place = lat_place(step)
        return pltpu.make_async_remote_copy(
            src_ref=mine_ref.at[other],
            dst_ref=coef_out.at[group, lat],
            send_sem=lat_send.at[step],
            recv_sem=lat_recv.at[step],
            device_id=place,
            device_id_type=MESH,
        )

    def sec_copy(step):
        return pltpu.make_async_remote_copy(
            src_ref=coef_out.at[group],
            dst_ref=coef_out.at[group],
            send_sem=sec_send.at[step],
            recv_sem=sec_recv.at[step],
            device_id={"sec": (sec + step) % sec_count, "lat": lat, "col": col},
            device_id_type=MESH,
        )

    def col_copy(back, step):
        block = (sec + sec_count - back) % sec_count * col_count + col
        return pltpu.make_async_remote_copy(
            src_ref=coef_out.at[block],
            dst_ref=coef_out.at[block],
            send_sem=col_send.at[back, step],
            recv_sem=col_recv.at[back, step],
            device_id={"sec": sec, "lat": lat, "col": (col + step) % col_count},
            device_id_type=MESH,
        )

    own_weights = pltpu.make_async_copy(weight_ref.at[group], weight_out.at[group], local_sem.at[0])
    own_weights.start()

    @pl.loop(1, groups)
    def _(step):
        weight_copy(step).start()

    @pl.when(has_next)
    def _():
        halo_copy(0).start()

    @pl.when(has_previous)
    def _():
        halo_copy(1).start()

    points = points_ref[0]
    waves = table_ref.shape[2]
    fields = x_ref.shape[0]
    chunks = x_ref.shape[1] // CHUNK
    low_c, low_s = table_ref[0, :LOW], table_ref[1, :LOW]
    for b in range(CHUNK // LOW):
        mid_c = table_ref[0, LOW + b : LOW + b + 1]
        mid_s = table_ref[1, LOW + b : LOW + b + 1]
        base_ref[0, b * LOW : (b + 1) * LOW] = low_c * mid_c - low_s * mid_s
        base_ref[1, b * LOW : (b + 1) * LOW] = low_c * mid_s + low_s * mid_c
    acc_ref[...] = jnp.zeros_like(acc_ref)
    top = LOW + CHUNK // LOW

    @pl.loop(0, chunks)
    def _(a):
        start = pl.multiple_of(a * CHUNK, CHUNK)
        position = start + lax.broadcasted_iota(jnp.int32, (fields, CHUNK), 1)
        block = x_ref[:, pl.ds(start, CHUNK)].astype(jnp.float32)
        block = jnp.where(position < points, block, 0.0).astype(jnp.bfloat16)
        high_c = table_ref[0, pl.ds(top + a, 1)]
        high_s = table_ref[1, pl.ds(top + a, 1)]
        for w in range(0, waves, 128):
            cut = slice(w, w + 128)
            base_c, base_s = base_ref[0, :, cut], base_ref[1, :, cut]
            turn_c, turn_s = high_c[:, cut], high_s[:, cut]
            real = (base_c * turn_c - base_s * turn_s).astype(jnp.bfloat16)
            imag = (base_c * turn_s + base_s * turn_c).astype(jnp.bfloat16)
            both = jnp.concatenate([real, imag], axis=1)
            part = jnp.dot(block, both, preferred_element_type=jnp.float32)
            acc_ref[:fields, cut] += part[:, :128]
            acc_ref[fields:, cut] += part[:, 128:]

    wave = lax.broadcasted_iota(jnp.int32, acc_ref.shape, 1)
    coefs = jnp.where(wave < points // 2, acc_ref[...], 0.0).astype(jnp.bfloat16)
    padded = mine_ref.shape[1]

    def fill(other):
        held = slots_ref[pl.ds(pl.multiple_of(other * padded, 16), padded)]
        pick = held == lax.broadcasted_iota(jnp.int32, (padded, waves), 1)
        pick = jnp.where(pick, 1.0, 0.0).astype(jnp.bfloat16)
        mine_ref[other] = lax.dot_general(
            pick, coefs, (((1,), (1,)), ((), ())), preferred_element_type=jnp.float32
        ).astype(jnp.bfloat16)

    @pl.loop(1, lat_count)
    def _(step):
        fill((lat + step) % lat_count)
        lat_copy(step).start()

    fill(lat)
    own_coefs = pltpu.make_async_copy(mine_ref.at[lat], coef_out.at[group, lat], local_sem.at[1])
    own_coefs.start()
    own_coefs.wait()

    @pl.loop(1, lat_count)
    def _(step):
        lat_copy(step).wait_recv()

    @pl.loop(1, sec_count)
    def _(step):
        sec_copy(step).start()

    @pl.loop(1, col_count)
    def _(step):
        col_copy(0, step).start()

    @pl.loop(1, sec_count)
    def _(back):
        sec_copy(back).wait_recv()

        @pl.loop(1, col_count)
        def _(step):
            col_copy(back, step).start()

    @pl.when(has_next)
    def _():
        halo_copy(0).wait_send()
        halo_copy(1).wait_recv()

    @pl.when(has_previous)
    def _():
        halo_copy(1).wait_send()
        halo_copy(0).wait_recv()

    own_weights.wait()

    @pl.loop(1, groups)
    def _(step):
        weight_copy(step).wait()

    @pl.loop(1, lat_count)
    def _(step):
        lat_copy(step).wait_send()

    @pl.loop(1, sec_count)
    def _(step):
        sec_copy(step).wait_send()

    @pl.loop(0, sec_count)
    def _(back):
        @pl.loop(1, col_count)
        def _(step):
            col_copy(back, step).wait()


def exchange(sizes, points, table, slots, state, weights, halo):
    fields, width = state.shape
    waves = table.shape[2]
    sec_count, lat_count, col_count = sizes
    groups = sec_count * col_count
    padded = weights.shape[1]
    anywhere = pl.BlockSpec(memory_space=pl.ANY)
    inside = pl.BlockSpec(memory_space=pltpu.VMEM)
    halo_shape = jax.ShapeDtypeStruct(halo.shape, halo.dtype)
    out = pl.pallas_call(
        functools.partial(exchange_kernel, sizes),
        out_shape=[
            jax.ShapeDtypeStruct((groups, lat_count, padded, 2 * fields), jnp.bfloat16),
            jax.ShapeDtypeStruct(weights.shape, jnp.bfloat16),
            halo_shape,
            halo_shape,
        ],
        in_specs=[pl.BlockSpec(memory_space=pltpu.SMEM), inside, inside, inside, anywhere, anywhere],
        out_specs=[anywhere] * 4,
        scratch_shapes=[
            pltpu.VMEM((2, CHUNK, waves), jnp.float32),
            pltpu.VMEM((2 * fields, waves), jnp.float32),
            pltpu.VMEM((lat_count, padded, 2 * fields), jnp.bfloat16),
            pltpu.SemaphoreType.DMA((2,)),
            pltpu.SemaphoreType.DMA((groups,)),
            pltpu.SemaphoreType.DMA((groups,)),
            pltpu.SemaphoreType.DMA((2,)),
            pltpu.SemaphoreType.DMA((2,)),
            pltpu.SemaphoreType.DMA((lat_count,)),
            pltpu.SemaphoreType.DMA((lat_count,)),
            pltpu.SemaphoreType.DMA((sec_count,)),
            pltpu.SemaphoreType.DMA((sec_count,)),
            pltpu.SemaphoreType.DMA((sec_count, col_count)),
            pltpu.SemaphoreType.DMA((sec_count, col_count)),
        ],
        compiler_params=pltpu.CompilerParams(
            vmem_limit_bytes=24 * 2**20, collective_id=0, has_side_effects=True
        ),
        cost_estimate=pl.CostEstimate(
            flops=4 * fields * waves * width, bytes_accessed=8 * 2**20, transcendentals=0
        ),
    )(points, table, slots, state, weights, halo)
    return out


REACH = (-2, -1, 1, 2)


def flux_kernel(sizes, row_ref, out_ref, send_sem, recv_sem):
    sec_count, lat_count, col_count = sizes
    devices = sec_count * lat_count * col_count
    sec, lat, col = (lax.axis_index(name) for name in LINE)
    line = (sec * lat_count + lat) * col_count + col
    places = [place_of((line + devices - step) % devices, lat_count, col_count) for step in REACH]
    barrier = pltpu.get_barrier_semaphore()
    for place in places:
        pl.semaphore_signal(barrier, inc=1, device_id=place, device_id_type=MESH)
    pl.semaphore_wait(barrier, len(REACH))
    copies = [
        pltpu.make_async_remote_copy(
            src_ref=row_ref,
            dst_ref=out_ref.at[k],
            send_sem=send_sem.at[k],
            recv_sem=recv_sem.at[k],
            device_id=place,
            device_id_type=MESH,
        )
        for k, place in enumerate(places)
    ]
    for copy in copies:
        copy.start()
    for copy in copies:
        copy.wait()


def near_rows(sizes, row):
    shape = (8, row.shape[0] // 8)
    out = pl.pallas_call(
        functools.partial(flux_kernel, sizes),
        out_shape=jax.ShapeDtypeStruct((len(REACH),) + shape, row.dtype),
        in_specs=[pl.BlockSpec(memory_space=pltpu.VMEM)],
        out_specs=pl.BlockSpec(memory_space=pltpu.VMEM),
        scratch_shapes=[pltpu.SemaphoreType.DMA((len(REACH),))] * 2,
        compiler_params=pltpu.CompilerParams(
            vmem_limit_bytes=2**20, collective_id=1, has_side_effects=True
        ),
    )(row.reshape(shape))
    return out.reshape(len(REACH), row.shape[0])


def legendre_kernel(degree_ref, slots_ref, weight_ref, coef_ref, out_ref):
    groups, lines, pair, width = coef_ref.shape
    rows = groups * lines
    packed = weight_ref.shape[2]
    degrees = out_ref.shape[1]
    first = degree_ref[0]
    for half in range(pair // 8):
        cut = slice(half * 8, half * 8 + 8)
        held = weight_ref[:, cut, :].astype(jnp.float32).reshape(groups * 8, packed)
        parts = [
            pltpu.roll(held, (packed - q * degrees) % packed, 1)[:, :128] if q else held[:, :128]
            for q in range(lines)
        ]
        values = jnp.concatenate(parts, axis=0).T[:degrees]
        lane_slot = lax.broadcasted_iota(jnp.int32, (degrees, rows * 8), 1) % 8
        coefs = jnp.concatenate(
            [
                coef_ref[:, q, cut, :].astype(jnp.float32).reshape(groups * 8, width)
                for q in range(lines)
            ],
            axis=0,
        ).astype(jnp.bfloat16)
        degree = first + lax.broadcasted_iota(jnp.int32, (degrees, width), 0)
        for s in range(8):
            wave = slots_ref[pl.program_id(0) * pair + half * 8 + s]
            left = jnp.where(lane_slot == s, values, 0.0).astype(jnp.bfloat16)
            summed = jnp.dot(left, coefs, preferred_element_type=jnp.float32)
            out_ref[half * 8 + s] = jnp.where(degree >= wave, summed, 0.0)


def legendre(weights, coefs, slots, first_degree, slot_count, degrees):
    groups, lines, padded, width = coefs.shape
    rows = groups * lines
    return pl.pallas_call(
        legendre_kernel,
        grid=(padded // SLOT_PAD,),
        out_shape=jax.ShapeDtypeStruct((slot_count, degrees, width), jnp.float32),
        in_specs=[
            pl.BlockSpec(memory_space=pltpu.SMEM),
            pl.BlockSpec(memory_space=pltpu.SMEM),
            pl.BlockSpec((groups, SLOT_PAD, weights.shape[2]), lambda i: (0, i, 0)),
            pl.BlockSpec((groups, lines, SLOT_PAD, width), lambda i: (0, 0, i, 0)),
        ],
        out_specs=pl.BlockSpec((SLOT_PAD, degrees, width), lambda i: (i, 0, 0)),
        compiler_params=pltpu.CompilerParams(vmem_limit_bytes=(8 if rows <= 64 else 32) * 2**20),
        cost_estimate=pl.CostEstimate(
            flops=2 * rows * padded * width * degrees * 8,
            bytes_accessed=4 * slot_count * degrees * width + 4 * rows * padded * width,
            transcendentals=0,
        ),
    )(first_degree, slots, weights, coefs)


def split_two(values):
    top = lax.reduce_precision(values, 8, 7)
    return [top.astype(jnp.bfloat16), (values - top).astype(jnp.bfloat16)]


def pick_points(arrays, index):
    length = arrays[0].shape[0]
    tiles = -(-length // 128)
    matrix = jnp.stack(arrays).reshape(len(arrays), tiles, 128)
    chosen = (jnp.arange(tiles, dtype=jnp.int32)[:, None] == index[None, :] // 128).astype(jnp.bfloat16)
    spread = jnp.einsum("kta,tx->kax", matrix, chosen, preferred_element_type=jnp.float32)
    lane = jnp.arange(128, dtype=jnp.int32)[:, None] == index[None, :] % 128
    return jnp.where(lane[None], spread, 0.0).sum(axis=1)


def advance_coupled_model(
    bordered_array,
    meridian_exchange_factor,
    zonal_exchange_factor,
    depthwise_exchange_factor,
    boundary_warming_term,
):
    centre = bordered_array[:, 1:-1]
    meridional = meridian_exchange_factor[1:] * (
        bordered_array[:, 2:] - centre
    ) - meridian_exchange_factor[:-1] * (centre - bordered_array[:, :-2])
    east_flux = zonal_exchange_factor * (jnp.roll(centre, -1, axis=2) - centre)
    zonal_div = east_flux - jnp.roll(east_flux, 1, axis=2)
    vertical_flux = depthwise_exchange_factor * (centre[1:] - centre[:-1])
    zero_layer = jnp.zeros_like(vertical_flux[:1])
    vertical = jnp.concatenate([vertical_flux, zero_layer], 0) - jnp.concatenate(
        [zero_layer, vertical_flux], 0
    )
    forced = jnp.concatenate([boundary_warming_term[None], jnp.zeros_like(centre[1:])], 0)
    return centre + meridional + zonal_div + vertical + forced


def body(
    physical_state,
    parallel_lengths,
    zonal_mode_assignment,
    weighted_associated_polynomials,
    marine_tracer_state,
    lateral_diffusivity,
    depthwise_diffusivity,
    water_indicator,
    overlying_parallel,
    underlying_marine_parallel,
):
    lat_count = lax.axis_size("lat")
    groups = lax.axis_size("sec") * lax.axis_size("col")
    devices = groups * lat_count
    grid_width = physical_state.shape[2]
    strata = physical_state.shape[1] // 4
    slot_count, wave_count, row_count = weighted_associated_polynomials.shape
    block_degrees = wave_count // groups
    padded = -(-slot_count // SLOT_PAD) * SLOT_PAD
    linear_index = (
        lax.axis_index("sec") * lat_count + lax.axis_index("lat")
    ) * lax.axis_size("col") + lax.axis_index("col")
    group_index = lax.axis_index("sec") * lax.axis_size("col") + lax.axis_index("col")
    points = parallel_lengths[0]

    rows = marine_tracer_state.shape[1]
    span = marine_tracer_state.shape[2]
    layers = marine_tracer_state.shape[0]
    relative = overlying_parallel - linear_index
    payload = jnp.concatenate(
        [
            marine_tracer_state,
            lateral_diffusivity[None],
            depthwise_diffusivity[None],
            water_indicator.astype(jnp.float32)[None],
            jnp.broadcast_to(relative.astype(jnp.float32)[:, None], (rows, span))[None],
        ],
        axis=0,
    )
    halo = payload.astype(jnp.bfloat16).reshape((layers + 4) * rows, span)

    send = weighted_associated_polynomials.reshape(slot_count, groups, block_degrees, row_count)
    send = jnp.transpose(send, (1, 0, 3, 2)).reshape(groups, slot_count, row_count * block_degrees)
    lanes = -(-send.shape[2] // 128) * 128
    send = jnp.pad(send, ((0, 0), (0, padded - slot_count), (0, lanes - send.shape[2])))
    slots = zonal_mode_assignment.reshape(lat_count, slot_count)
    slots = jnp.pad(slots, ((0, 0), (0, padded - slot_count)), constant_values=wave_count)
    coefs, weights, before, after = exchange(
        (lax.axis_size("sec"), lat_count, lax.axis_size("col")),
        parallel_lengths,
        angle_tables(points, wave_count, grid_width),
        slots.reshape(-1, 1),
        physical_state[0],
        send,
        halo,
    )
    first, last = linear_index == 0, linear_index == devices - 1
    before = jnp.where(first, jnp.zeros_like(before), before).astype(jnp.float32)
    after = jnp.where(last, jnp.zeros_like(after), after).astype(jnp.float32)
    before = before.reshape(payload.shape)
    after = after.reshape(payload.shape)

    surface = jnp.concatenate([before[0], marine_tracer_state[0], after[0]], axis=0)
    under = underlying_marine_parallel[0] - (linear_index - 1) * rows
    skin = jnp.where(jnp.arange(3 * rows)[:, None] == under, surface, 0.0).sum(axis=0)
    ocean_points = jnp.arange(span, dtype=jnp.int32)
    column = ocean_points * points // span
    sea_column = jnp.minimum(column * span // points, span - 1)
    skin_hi, skin_lo = split_two(skin)
    mapped = pick_points([skin_hi, skin_lo], sea_column)
    bottom = strata - 1
    zonal_wind = physical_state[0, bottom].astype(jnp.float32)
    meridional_wind = physical_state[0, strata + bottom].astype(jnp.float32)
    speed = thermal_transfer_factor * jnp.sqrt(
        zonal_wind * zonal_wind + meridional_wind * meridional_wind + 1.0
    )
    speed_hi, speed_lo = split_two(speed)
    picked = pick_points([speed_hi, speed_lo, physical_state[0, 2 * strata + bottom]], column)
    flux = (picked[0] + picked[1]) * (mapped[0] + mapped[1] - picked[2])
    near = near_rows((lax.axis_size("sec"), lat_count, lax.axis_size("col")), flux)
    flux_near = {0: flux, **{step: near[k] for k, step in enumerate(REACH)}}

    whole = jnp.concatenate([before, payload, after], axis=1)
    thermal = whole[:layers]
    kappa, depth, sea, relative = (whole[layers + k] for k in range(4))
    owner = jnp.arange(3 * rows, dtype=jnp.int32)[:, None] // rows - 1
    target = relative + owner.astype(jnp.float32)
    forcing = jnp.zeros_like(sea)
    for step, row in flux_near.items():
        forcing = jnp.where(target == step, row[None], forcing)
    source = force_coef * sea * forcing
    depthwise = depth * sea
    faces = 0.5 * (kappa[:-1] + kappa[1:]) * sea[:-1] * sea[1:]
    east = 0.5 * (kappa + jnp.roll(kappa, -1, axis=1)) * sea * jnp.roll(sea, -1, axis=1)
    total = 3 * rows
    for iteration in range(OSTEPS):
        a, b = iteration + 1, total - iteration - 1
        thermal = advance_coupled_model(
            thermal, faces[a - 1 : b], east[a:b], depthwise[a:b], source[a:b]
        )

    own_waves = lax.dynamic_slice_in_dim(
        slots.reshape(-1), lax.axis_index("lat") * padded, padded
    )
    first_degree = jnp.reshape(group_index * block_degrees, (1,)).astype(jnp.int32)
    harmonic = legendre(weights, coefs, own_waves, first_degree, slot_count, block_degrees)
    return (jnp.transpose(harmonic, (1, 0, 2)), thermal)


def solution(mesh):
    return jax.shard_map(
        body,
        mesh=mesh,
        in_specs=(
            P(LINE, None, None),
            P(LINE),
            P(),
            P("lat", None, GROUP),
            P(None, LINE, None),
            P(LINE, None),
            P(LINE, None),
            P(LINE, None),
            P(LINE),
            P(LINE),
        ),
        out_specs=(P(GROUP, "lat", None), P(None, LINE, None)),
        check_vma=False,
    )
```

profile of v0, /device:TPU:0, one launch (start us, length us, event | category | flops | bytes accessed | tf_op | source)
XLA Modules:
  0.0 94.8 jit_solution(4759474989079382854)
XLA Ops:
  3.0 1.1 %constant_dynamic-update-slice_fusion = f32[12,4,4096]{2,1,0:T(4,128)S(1)} fusion(f32[8,4,4096]{2,1,0:T(4,128)} %param.14), kind=kLoop, calls=%fused_computation.163 | loop fusion | bytes 1048576
  4.3 0.9 copy-done.4
  5.9 2.6 %copy.13 = bf16[214,640,4]{0,1,2:T(8,128)(2,1)S(1)} copy(bf16[214,640,4]{1,2,0:T(4,128)(2,1)} %param.13) | data formatting | bytes 2191360 | tf_op args[3]
  8.5 1.2 %copy.14 = bf16[8,214,4,80]{1,3,2,0:T(8,128)(2,1)} copy(bf16[8,214,4,80]{1,3,0,2:T(8,128)(2,1)S(1)} %bitcast.102) | data formatting | bytes 2191360 | tf_op jit(solution)/shard_map/transpose | solution.py:488
  9.7 1.8 %copy.15 = bf16[8,214,320]{2,1,0:T(8,128)(2,1)S(1)} copy(bf16[8,214,320]{1,2,0:T(8,128)(2,1)} %bitcast.101) | data formatting | bytes 2191360 | tf_op jit(solution)/shard_map/reshape | solution.py:488
  11.6 0.9 copy-done.2
  12.5 37.6 %shard_map.113 = (bf16[8,4,224,128]{3,2,1,0:T(8,128)(2,1)S(1)}, bf16[8,224,384]{2,1,0:T(8,128)(2,1)S(1)}, bf16[48,4096]{1,0:T(8,128)(2,1)S(1)}, bf16[48,4096]{1,0:T(8,128)(2,1)S(1)}) custom-call(s32[1]{0:T(128)} %copy.25.points_ref, f32[2,60,640]{2,1,0:T(8,128)S(1)} %maximum_multiply_fusion.table_ref, s32[896,1]{1,0:T(8,128)S(1)} %reshape.506.slots_ref, ...), custom_call_target="tpu_custom_call" | custom-call | flops 838860800 | bytes 8388608 | tf_op jit(solution)/shard_map/pallas_call | solution.py:274
  50.2 1.1 %copy-done = bf16[8,224,384]{2,1,0:T(8,128)(2,1)} copy-done((bf16[8,224,384]{2,1,0:T(8,128)(2,1)}, bf16[8,224,384]{2,1,0:T(8,128)(2,1)S(1)}, u32[]{:S(2)}) %copy-start) | copy-done | bytes 1376280
  51.3 0.7 copy-done.3
  52.0 1.1 %select_convert_fusion = (f32[48,4096]{1,0:T(8,128)S(1)}, f32[48,4096]{1,0:T(8,128)S(1)}) fusion(bf16[48,4096]{1,0:T(8,128)(2,1)} %copy-done.3, pred[]{:T(512)S(6)} %eq.108, bf16[48,4096]{1,0:T(8,128)(2,1)S(1)} %get-tuple-element.8, pred[]{:T(512)S(6)} %eq.107), kind=kLoop, calls=%fused_computation.69 | loop fusion | flops 786432 | bytes 2359298 | tf_op jit(solution)/shard_map/convert_element_type | solution.py:504
  53.1 0.9 copy-done.8
  54.7 0.8 slice_bitcast_fusion.16
  56.2 0.9 fusion.11
  57.5 1.0 %sqrt_multiply_fusion = f32[1,1,5120]{2,1,0:T(1,128)S(1)} fusion(bf16[1,64,5120]{2,1,0:T(8,128)(2,1)} %param.10), kind=kLoop, calls=%fused_computation.136 | loop fusion | flops 35840 | bytes 40960 | tf_op jit(solution)/shard_map/mul | solution.py:519
  58.5 1.0 %slice_reduce_fusion = bf16[5120]{0:T(1024)(128)(2,1)S(1)} fusion(bf16[1,64,5120]{2,1,0:T(8,128)(2,1)} %param.10), kind=kLoop, calls=%fused_computation.137 | loop fusion | bytes 20480 | tf_op jit(solution)/shard_map/slice | solution.py:523
  59.5 1.2 %select_reduce_fusion = f32[3,4096]{1,0:T(4,128)S(1)} fusion(pred[128,4096]{1,0:T(8,128)(4,1)S(1)} %iota_compare_fusion.1, s32[4096]{0:T(1024)S(1)} %get-tuple-element.37, bf16[1,40,128]{2,1,0:T(8,128)(2,1)S(1)} %bitcast.110, bf16[1,40,128]{2,1,0:T(8,128)(2,1)S(1)} %get-tuple-element.30, bf16[1,40,128]{2,1,0:T(8,128)(2,1)S(1)} %get-tuple-element.29), kind=kOutput, calls=%fused_computation | convolution fusion | flops 129157120 | bytes 620544 | tf_op jit(solution)/shard_map/kta,tx->kax/dot_general | solution.py:418
  61.2 0.7 fusion.77
  62.0 7.5 %shard_map.115 = f32[4,8,512]{2,1,0:T(8,128)S(1)} custom-call(f32[8,512]{1,0:T(8,128)S(1)} %mul.393.row_ref), custom_call_target="tpu_custom_call" | custom-call | tf_op jit(solution)/shard_map/pallas_call | solution.py:342
  69.6 1.4 %reshape.499 = f32[12,4,4096]{2,1,0:T(4,128)S(1)} reshape(f32[48,4096]{1,0:T(8,128)} %copy-done.8) | data formatting | bytes 1572864 | tf_op jit(solution)/shard_map/reshape | solution.py:505
  70.9 2.2 %reshape.500 = f32[12,4,4096]{2,1,0:T(4,128)} reshape(f32[48,4096]{1,0:T(8,128)} %copy-done.7) | data formatting | bytes 1572864 | tf_op jit(solution)/shard_map/reshape | solution.py:506
  73.2 1.7 %pad_maximum_fusion = f32[12,12,4096]{2,1,0:T(8,128)S(1)} fusion(f32[12,4,4096]{2,1,0:T(4,128)} %reshape.500, f32[12,4,4096]{2,1,0:T(4,128)S(1)} %copy-done.5, f32[12,4,4096]{2,1,0:T(4,128)S(1)} %reshape.499), kind=kLoop, calls=%fused_computation.2 | loop fusion | flops 1179648 | bytes 4718592 | tf_op jit(solution)/shard_map/concatenate | solution.py:528
  77.5 1.7 %fusion.8 = f32[8,10,4096]{2,1,0:T(8,128)S(1)} fusion(f32[12,12,4096]{2,1,0:T(8,128)S(1)} %pad_maximum_fusion, f32[8,10,4096]{2,1,0:T(8,128)S(1)} %fusion.2, f32[8,10,4095]{2,1,0:T(8,128)S(1)} %bitcast.97, f32[8,10,1]{2,1,0:T(8,128)S(1)} %slice.442, f32[1,10,4096]{2,1,0:T(8,128)S(1)} %slice_bitcast_fusion, f32[7,10,4096]{2,1,0:T(8,128)S(1)} %fusion.10, ...), kind=kLoop, calls=%fused_computation.14 | loop fusion | flops 3932160 | bytes 9502720 | tf_op jit(solution)/shard_map/add | solution.py:442
  83.1 1.4 %fusion.37 = f32[8,4,4096]{2,1,0:T(4,128)} fusion(f32[8,6,4096]{2,1,0:T(8,128)S(1)} %fusion.17, f32[8,4,4096]{2,1,0:T(4,128)S(1)} %fusion.39, f32[8,4,4095]{2,1,0:T(4,128)S(1)} %bitcast.103, f32[8,4,1]{2,1,0:T(4,128)S(1)} %slice.493, f32[1,4,4096]{2,1,0:T(4,128)S(1)} %slice_bitcast_fusion.13, f32[7,4,4096]{2,1,0:T(4,128)S(1)} %fusion.42, ...), kind=kLoop, calls=%fused_computation.59 | loop fusion | flops 1572864 | bytes 3801088 | tf_op jit(solution)/shard_map/add | solution.py:442
  84.6 10.2 %shard_map.114 = f32[214,80,128]{2,1,0:T(8,128)} custom-call(s32[1]{0:T(128)} %bitcast.degree_ref, s32[224]{0:T(256)S(1)} %dynamic_slice.3.slots_ref, bf16[8,224,384]{2,1,0:T(8,128)(2,1)S(1)} %copy-done.1, bf16[8,4,224,128]{3,2,1,0:T(8,128)(2,1)S(1)} %get-tuple-element.7.coef_ref), custom_call_target="tpu_custom_call" | custom-call | flops 1174405120 | bytes 12435456 | tf_op jit(solution)/shard_map/pallas_call | solution.py:388
  (103 shorter events, 10.5 us)
Async XLA Ops:
  0.6 3.5 %copy-start.9 = (f32[4,4096]{1,0:T(4,128)S(1)}, f32[4,4096]{1,0:T(4,128)}, u32[]{:S(2)}) copy-start(f32[4,4096]{1,0:T(4,128)} %param.15) | copy-start | bytes 196612
  0.6 3.5 %copy-start.10 = (f32[4,4096]{1,0:T(4,128)S(1)}, f32[4,4096]{1,0:T(4,128)}, u32[]{:S(2)}) copy-start(f32[4,4096]{1,0:T(4,128)} %param.16) | copy-start | bytes 196612
  0.7 3.5 %copy-start.11 = (s32[4,4096]{1,0:T(4,128)S(1)}, s32[4,4096]{1,0:T(4,128)}, u32[]{:S(2)}) copy-start(s32[4,4096]{1,0:T(4,128)} %param.17) | copy-start | bytes 196612
  2.2 3.3 %copy-start.12 = (s32[856]{0:T(1024)S(1)}, s32[856]{0:T(1024)}, u32[]{:S(2)}) copy-start(s32[856]{0:T(1024)} %param.12) | copy-start | bytes 10276
  4.3 0.9 copy-start.4
  11.5 1.1 %copy-start.2 = (bf16[1,64,5120]{2,1,0:T(8,128)(2,1)S(1)}, bf16[1,64,5120]{2,1,0:T(8,128)(2,1)}, u32[]{:S(2)}) copy-start(bf16[1,64,5120]{2,1,0:T(8,128)(2,1)} %param.10) | copy-start | bytes 1966084
  50.2 1.1 %copy-start = (bf16[8,224,384]{2,1,0:T(8,128)(2,1)}, bf16[8,224,384]{2,1,0:T(8,128)(2,1)S(1)}, u32[]{:S(2)}) copy-start(bf16[8,224,384]{2,1,0:T(8,128)(2,1)S(1)} %get-tuple-element.6.weight_ref) | copy-start | bytes 4128772
  51.3 0.7 copy-start.3
  53.1 0.9 copy-start.8
  53.1 4.0 %copy-start.7 = (f32[48,4096]{1,0:T(8,128)}, f32[48,4096]{1,0:T(8,128)S(1)}, u32[]{:S(2)}) copy-start(f32[48,4096]{1,0:T(8,128)S(1)} %get-tuple-element.39) | copy-start | bytes 2359300
  60.7 12.5 %copy-start.5 = (f32[12,4,4096]{2,1,0:T(4,128)S(1)}, f32[12,4,4096]{2,1,0:T(4,128)}, u32[]{:S(2)}) copy-start(f32[12,4,4096]{2,1,0:T(4,128)} %copy-done.4) | copy-start | bytes 2359300
  75.8 1.1 %copy-start.6 = (f32[12,4,4096]{2,1,0:T(4,128)S(1)}, f32[12,4,4096]{2,1,0:T(4,128)}, u32[]{:S(2)}) copy-start(f32[12,4,4096]{2,1,0:T(4,128)} %reshape.500) | copy-start | bytes 2359300
  83.1 1.6 %copy-start.1 = (bf16[8,224,384]{2,1,0:T(8,128)(2,1)S(1)}, bf16[8,224,384]{2,1,0:T(8,128)(2,1)}, u32[]{:S(2)}) copy-start(bf16[8,224,384]{2,1,0:T(8,128)(2,1)} %copy-done) | copy-start | bytes 4128772
where the time goes:
time: 95.5 us; the launch traced here: 94.8 us
  Pallas kernels  55.3 us (58%)
  local copies, waits for them, and re-layouts  21.1 us (22%)
  other arithmetic  13.4 us (14%)
  between operations  2.75 us (3%)
  matrix products  2.12 us (2%)
    pallas_call x1, Pallas kernels, exchange(): pl.pallas_call(functools.partial(exchange_kernel, sizes), out_shape=[jax....  37.6 us
    pallas_call x1, Pallas kernels, legendre(): pl.pallas_call(legendre_kernel, grid=(padded // SLOT_PAD,), out_shape=jax...  10.2 us
    unnamed x35, local copies, waits for them, and re-layouts  8.77 us
    pallas_call x1, Pallas kernels, near_rows(): pl.pallas_call(functools.partial(flux_kernel, sizes), out_shape=jax.Shape...  7.55 us
    add x4, other arithmetic, advance_coupled_model(): return centre + meridional + zonal_div + vertical + forced  4.27 us
    reshape x1, local copies, waits for them, and re-layouts, body(): after = after.reshape(payload.shape)  2.23 us
    dot_general x2, matrix products, pick_points(): jnp.einsum('kta,tx->kax', matrix, chosen, preferred_element_type=jnp.floa...  2.12 us

commit v1 on v0

--- a/solution.py
+++ b/solution.py
@@ -552,9 +552,678 @@
     return (jnp.transpose(harmonic, (1, 0, 2)), thermal)
 
 
+def fast_kernel(
+    sizes,
+    points_ref,
+    over_ref,
+    under_ref,
+    table_ref,
+    slots_ref,
+    x_ref,
+    weight_ref,
+    kappa_ref,
+    depth_ref,
+    water_ref,
+    ocean_ref,
+    coef_out,
+    weight_out,
+    thermal_out,
+    msg_ref,
+    base_ref,
+    xm_ref,
+    z_ref,
+    coefs_ref,
+    mine_ref,
+    halo_ref,
+    before_ref,
+    after_ref,
+    plane_ref,
+    heat_ref,
+    face_ref,
+    east_ref,
+    down_ref,
+    source_ref,
+    local_ref,
+    flux_ref,
+    ocean_sem,
+    local_sem,
+    weight_send,
+    weight_recv,
+    halo_send,
+    halo_recv,
+    flux_send,
+    flux_recv,
+    lat_send,
+    lat_recv,
+    direct_send,
+    direct_recv,
+    diag_send,
+    diag_recv,
+    chip_send,
+    chip_recv,
+):
+    sec_count, lat_count, col_count = sizes
+    groups = sec_count * col_count
+    devices = groups * lat_count
+    sec, lat, col = (lax.axis_index(name) for name in LINE)
+    group = sec * col_count + col
+    line = (sec * lat_count + lat) * col_count + col
+    rows, layers, span = thermal_out.shape
+    following = place_of((line + 1) % devices, lat_count, col_count)
+    previous = place_of((line + devices - 1) % devices, lat_count, col_count)
+    has_next, has_previous = line < devices - 1, line > 0
+    sides = (sec + 1 - 2 * (sec % 2), (sec + 2) % 4)
+    corner = 3 - sec
+
+    ocean_copies = [
+        pltpu.make_async_copy(ocean_ref.at[:, r, :], heat_ref.at[0, rows + r], ocean_sem.at[r])
+        for r in range(rows)
+    ]
+    for copy in ocean_copies:
+        copy.start()
+
+    def group_place(step):
+        other = (group + step) % groups
+        return other, {"sec": other // col_count, "lat": lat, "col": other % col_count}
+
+    def lat_place(step):
+        other = (lat + step) % lat_count
+        return other, {"sec": sec, "lat": other, "col": col}
+
+    flux_places = [place_of((line + devices - step) % devices, lat_count, col_count) for step in REACH]
+    barrier = pltpu.get_barrier_semaphore()
+    for place in flux_places:
+        pl.semaphore_signal(barrier, inc=1, device_id=place, device_id_type=MESH)
+
+    @pl.loop(1, groups)
+    def _(step):
+        pl.semaphore_signal(barrier, inc=1, device_id=group_place(step)[1], device_id_type=MESH)
+
+    @pl.loop(1, lat_count)
+    def _(step):
+        pl.semaphore_signal(barrier, inc=1, device_id=lat_place(step)[1], device_id_type=MESH)
+
+    def weight_copy(step):
+        other, place = group_place(step)
+        return pltpu.make_async_remote_copy(
+            src_ref=msg_ref.at[other],
+            dst_ref=weight_out.at[group],
+            send_sem=weight_send.at[step],
+            recv_sem=weight_recv.at[step],
+            device_id=place,
+            device_id_type=MESH,
+        )
+
+    def halo_copy(side):
+        return pltpu.make_async_remote_copy(
+            src_ref=halo_ref,
+            dst_ref=(before_ref, after_ref)[side],
+            send_sem=halo_send.at[side],
+            recv_sem=halo_recv.at[side],
+            device_id=(following, previous)[side],
+            device_id_type=MESH,
+        )
+
+    def flux_copy(k):
+        return pltpu.make_async_remote_copy(
+            src_ref=flux_ref.at[len(REACH)],
+            dst_ref=flux_ref.at[k],
+            send_sem=flux_send.at[k],
+            recv_sem=flux_recv.at[k],
+            device_id=flux_places[k],
+            device_id_type=MESH,
+        )
+
+    def lat_copy(step):
+        other, place = lat_place(step)
+        return pltpu.make_async_remote_copy(
+            src_ref=mine_ref.at[other],
+            dst_ref=coef_out.at[group, lat],
+            send_sem=lat_send.at[step],
+            recv_sem=lat_recv.at[step],
+            device_id=place,
+            device_id_type=MESH,
+        )
+
+    def direct_copy(side, line_row):
+        piece = coef_out.at[group, line_row]
+        return pltpu.make_async_remote_copy(
+            src_ref=piece,
+            dst_ref=piece,
+            send_sem=direct_send.at[side, line_row],
+            recv_sem=direct_recv.at[side, line_row],
+            device_id={"sec": sides[side], "lat": lat, "col": col},
+            device_id_type=MESH,
+        )
+
+    def diag_copy(side, line_row):
+        piece = coef_out.at[sides[side] * col_count + col, line_row]
+        return pltpu.make_async_remote_copy(
+            src_ref=piece,
+            dst_ref=piece,
+            send_sem=diag_send.at[line_row],
+            recv_sem=diag_recv.at[line_row],
+            device_id={"sec": sides[1 - side], "lat": lat, "col": col},
+            device_id_type=MESH,
+        )
+
+    def chip_copy(which, line_row):
+        origin = (sec, sides[0], sides[1], corner)[which]
+        piece = coef_out.at[origin * col_count + col, line_row]
+        return pltpu.make_async_remote_copy(
+            src_ref=piece,
+            dst_ref=piece,
+            send_sem=chip_send.at[which, line_row],
+            recv_sem=chip_recv.at[which, line_row],
+            device_id={"sec": sec, "lat": lat, "col": 1 - col},
+            device_id_type=MESH,
+        )
+
+    band = msg_ref.shape[1]
+    degrees = msg_ref.shape[2] // groups
+    halves = weight_ref.shape[1] // band
+    for g in range(groups):
+        for p in range(groups):
+            t, h = p // halves, p % halves
+            msg_ref[g, :, p * degrees : (p + 1) * degrees] = weight_ref[
+                t, h * band : (h + 1) * band, g * degrees : (g + 1) * degrees
+            ]
+
+    pl.semaphore_wait(barrier, len(REACH) + groups - 1 + lat_count - 1)
+
+    @pl.loop(1, groups)
+    def _(step):
+        weight_copy(step).start()
+
+    own_weights = pltpu.make_async_copy(msg_ref.at[group], weight_out.at[group], local_sem.at[0])
+    own_weights.start()
+
+    sea = water_ref[...].astype(jnp.float32)
+    plane_ref[0:rows] = kappa_ref[...] * sea
+    plane_ref[rows : 2 * rows] = depth_ref[...] * sea
+    row_index = lax.broadcasted_iota(jnp.int32, (rows, span), 0)
+    relative = jnp.zeros((rows, span), jnp.float32)
+    for r in range(rows):
+        relative = jnp.where(row_index == r, (over_ref[r] - line).astype(jnp.float32), relative)
+    plane_ref[2 * rows : 3 * rows] = relative
+    plane_ref[3 * rows : 4 * rows] = relative
+    halo_ref[rows * layers :] = plane_ref[...].astype(jnp.bfloat16)
+    for copy in ocean_copies:
+        copy.wait()
+    for r in range(0, rows, 2):
+        pair = jnp.concatenate([heat_ref[0, rows + r], heat_ref[0, rows + r + 1]], axis=0)
+        halo_ref[r * layers : (r + 2) * layers] = pair.astype(jnp.bfloat16)
+
+    @pl.when(has_next)
+    def _():
+        halo_copy(0).start()
+
+    @pl.when(has_previous)
+    def _():
+        halo_copy(1).start()
+
+    points = points_ref[0]
+    waves = table_ref.shape[2]
+    fields = x_ref.shape[0]
+    chunks = x_ref.shape[1] // CHUNK
+    low_c, low_s = table_ref[0, :LOW], table_ref[1, :LOW]
+    for w in range(waves // 128):
+        cut = slice(w * 128, w * 128 + 128)
+        for b in range(0, CHUNK // LOW, 2):
+            real, imag = [], []
+            for q in (b, b + 1):
+                mid_c = table_ref[0, LOW + q : LOW + q + 1, cut]
+                mid_s = table_ref[1, LOW + q : LOW + q + 1, cut]
+                real.append(low_c[:, cut] * mid_c - low_s[:, cut] * mid_s)
+                imag.append(low_c[:, cut] * mid_s + low_s[:, cut] * mid_c)
+            real = jnp.concatenate(real, axis=0).astype(jnp.bfloat16)
+            imag = jnp.concatenate(imag, axis=0).astype(jnp.bfloat16)
+            base_ref[w, b * LOW : (b + 2) * LOW, :128] = real
+            base_ref[w, b * LOW : (b + 2) * LOW, 128:] = imag
+    for a in range(chunks):
+        position = a * CHUNK + lax.broadcasted_iota(jnp.int32, (fields, CHUNK), 1)
+        block = x_ref[:, a * CHUNK : (a + 1) * CHUNK].astype(jnp.float32)
+        xm_ref[a * fields : (a + 1) * fields] = jnp.where(position < points, block, 0.0).astype(
+            jnp.bfloat16
+        )
+    top = LOW + CHUNK // LOW
+    for w in range(waves // 128):
+        cut = slice(w * 128, w * 128 + 128)
+        z_ref[...] = jnp.dot(xm_ref[...], base_ref[w], preferred_element_type=jnp.float32)
+        real = jnp.zeros((fields, 128), jnp.float32)
+        imag = jnp.zeros((fields, 128), jnp.float32)
+        for a in range(chunks):
+            turn_c = table_ref[0, top + a : top + a + 1, cut]
+            turn_s = table_ref[1, top + a : top + a + 1, cut]
+            part_r = z_ref[a * fields : (a + 1) * fields, :128]
+            part_i = z_ref[a * fields : (a + 1) * fields, 128:]
+            real = real + part_r * turn_c - part_i * turn_s
+            imag = imag + part_r * turn_s + part_i * turn_c
+        wave = w * 128 + lax.broadcasted_iota(jnp.int32, (fields, 128), 1)
+        kept = wave < points // 2
+        coefs_ref[:fields, cut] = jnp.where(kept, real, 0.0).astype(jnp.bfloat16)
+        coefs_ref[fields:, cut] = jnp.where(kept, imag, 0.0).astype(jnp.bfloat16)
+    padded = mine_ref.shape[1]
+
+    def fill(other):
+        held = slots_ref[pl.ds(pl.multiple_of(other * padded, 16), padded)]
+        pick = held == lax.broadcasted_iota(jnp.int32, (padded, waves), 1)
+        pick = jnp.where(pick, 1.0, 0.0).astype(jnp.bfloat16)
+        mine_ref[other] = lax.dot_general(
+            pick, coefs_ref[...], (((1,), (1,)), ((), ())), preferred_element_type=jnp.float32
+        ).astype(jnp.bfloat16)
+
+    @pl.loop(1, lat_count)
+    def _(step):
+        fill((lat + step) % lat_count)
+        lat_copy(step).start()
+
+    fill(lat)
+    own_coefs = pltpu.make_async_copy(mine_ref.at[lat], coef_out.at[group, lat], local_sem.at[1])
+    own_coefs.start()
+
+    def spread_piece(line_row):
+        direct_copy(0, line_row).start()
+        direct_copy(1, line_row).start()
+        chip_copy(0, line_row).start()
+
+    own_coefs.wait()
+    spread_piece(lat)
+
+    strata = fields // 4
+    bottom = strata - 1
+    wide = 512
+    shift = span.bit_length() - 1
+
+    def halves_of(value):
+        upper = value.astype(jnp.bfloat16).astype(jnp.float32)
+        return upper, value - upper
+
+    def columns_of(start):
+        place = start + lax.broadcasted_iota(jnp.int32, (1, wide), 1)
+        return lax.shift_right_logical(place * points, shift)
+
+    def pick(table, index):
+        tiles = table.shape[1]
+        one = lax.broadcasted_iota(jnp.int32, (tiles, wide), 0) == lax.shift_right_logical(index, 7)
+        one = jnp.where(one, 1.0, 0.0).astype(jnp.bfloat16)
+        lane = lax.broadcasted_iota(jnp.int32, (128, wide), 0) == (index & 127)
+        spread = jnp.dot(table, one, preferred_element_type=jnp.float32)
+        return [
+            jnp.sum(jnp.where(lane, spread[k * 128 : (k + 1) * 128], 0.0), axis=0, keepdims=True)
+            for k in range(table.shape[0] // 128)
+        ]
+
+    def table_of(values):
+        tiles = values[0].shape[1] // 128
+        return jnp.concatenate([v.reshape(tiles, 128).T for v in values], axis=0).astype(jnp.bfloat16)
+
+    zonal = x_ref[bottom : bottom + 1].astype(jnp.float32)
+    meridional = x_ref[strata + bottom : strata + bottom + 1].astype(jnp.float32)
+    air = x_ref[2 * strata + bottom : 2 * strata + bottom + 1].astype(jnp.float32)
+    speed = thermal_transfer_factor * jnp.sqrt(zonal * zonal + meridional * meridional + 1.0)
+    table = table_of([*halves_of(speed), air])
+
+    @pl.loop(0, span // wide)
+    def _(k):
+        start = pl.multiple_of(k * wide, wide)
+        upper, lower, below = pick(table, columns_of(start))
+        local_ref[0:1, pl.ds(start, wide)] = upper + lower
+        local_ref[1:2, pl.ds(start, wide)] = below
+
+    @pl.when(has_next)
+    def _():
+        halo_copy(0).wait_send()
+        halo_copy(1).wait_recv()
+
+    @pl.when(has_previous)
+    def _():
+        halo_copy(1).wait_send()
+        halo_copy(0).wait_recv()
+
+    @pl.when(jnp.logical_not(has_next))
+    def _():
+        after_ref[...] = jnp.zeros_like(after_ref)
+
+    @pl.when(jnp.logical_not(has_previous))
+    def _():
+        before_ref[...] = jnp.zeros_like(before_ref)
+
+    for r in range(0, rows, 2):
+        for start, held in ((0, before_ref), (2 * rows, after_ref)):
+            pair = held[r * layers : (r + 2) * layers].astype(jnp.float32)
+            heat_ref[0, start + r] = pair[:layers]
+            heat_ref[0, start + r + 1] = pair[layers:]
+
+    under = under_ref[0] - (line - 1) * rows
+    skin = jnp.zeros((1, span), jnp.float32)
+    for r in range(3 * rows):
+        skin = jnp.where(under == r, heat_ref[0, r, 0:1, :], skin)
+    skin_table = table_of(halves_of(skin))
+    inverse = 1.0 / jnp.full((1, wide), points, jnp.int32).astype(jnp.float32)
+
+    @pl.loop(0, span // wide)
+    def _(k):
+        start = pl.multiple_of(k * wide, wide)
+        scaled = columns_of(start) << shift
+        index = (scaled.astype(jnp.float32) * inverse).astype(jnp.int32)
+        rest = scaled - index * points
+        index = jnp.where(rest < 0, index - 1, jnp.where(rest >= points, index + 1, index))
+        index = jnp.minimum(index, span - 1)
+        upper, lower = pick(skin_table, index)
+        cut = pl.ds(start, wide)
+        flux_ref[len(REACH), 0:1, cut] = local_ref[0:1, cut] * (upper + lower - local_ref[1:2, cut])
+
+    for k in range(len(REACH)):
+        flux_copy(k).start()
+
+    @pl.loop(1, lat_count)
+    def _(step):
+        lat_copy(step).wait_recv()
+        spread_piece((lat + lat_count - step) % lat_count)
+
+    edges = [before_ref[rows * layers :].astype(jnp.float32), after_ref[rows * layers :].astype(jnp.float32)]
+    centre = plane_ref[...]
+    kappa = jnp.concatenate([edges[0][:rows], centre[:rows], edges[1][:rows]], axis=0)
+    depth = jnp.concatenate([edges[0][rows : 2 * rows], centre[rows : 2 * rows], edges[1][rows : 2 * rows]], axis=0)
+    reach = jnp.concatenate(
+        [edges[0][2 * rows : 3 * rows] - 1.0, centre[2 * rows : 3 * rows], edges[1][2 * rows : 3 * rows] + 1.0],
+        axis=0,
+    )
+    total = 3 * rows
+    layer = lax.broadcasted_iota(jnp.int32, (layers, span), 0)
+    beside = pltpu.roll(kappa, span - 1, 1)
+    east = jnp.where((kappa > 0.0) & (beside > 0.0), 0.5 * (kappa + beside), 0.0)
+    upper, lower = kappa[:-1], kappa[1:]
+    faces = jnp.where((upper > 0.0) & (lower > 0.0), 0.5 * (upper + lower), 0.0)
+    for r in range(1, total):
+        face_ref[r] = jnp.broadcast_to(faces[r - 1 : r], (layers, span))
+    for r in range(1, total - 1):
+        east_ref[r] = jnp.broadcast_to(east[r : r + 1], (layers, span))
+        down_ref[r] = jnp.where(layer < layers - 1, depth[r : r + 1], 0.0)
+
+    for k in range(len(REACH)):
+        flux_copy(k).wait()
+    forcing = jnp.zeros_like(kappa)
+    for k, step in enumerate(REACH + (0,)):
+        forcing = jnp.where(reach == float(step), flux_ref[k], forcing)
+    forcing = jnp.where(kappa > 0.0, force_coef * forcing, 0.0)
+    for r in range(1, total - 1):
+        source_ref[r] = jnp.where(layer == 0, forcing[r : r + 1], 0.0)
+
+    for step in range(OSTEPS):
+        held, made = step % 2, (step + 1) % 2
+
+        @pl.loop(step + 1, total - step - 1)
+        def _(r):
+            mid = heat_ref[held, r]
+            flow = face_ref[r + 1] * (heat_ref[held, r + 1] - mid) - face_ref[r] * (mid - heat_ref[held, r - 1])
+            lateral = east_ref[r] * (pltpu.roll(mid, span - 1, 1) - mid)
+            flow = flow + (lateral - pltpu.roll(lateral, 1, 1))
+            sinking = down_ref[r] * (pltpu.roll(mid, layers - 1, 0) - mid)
+            flow = flow + (sinking - pltpu.roll(sinking, 1, 0))
+            fresh = mid + flow + source_ref[r]
+            if step < OSTEPS - 1:
+                heat_ref[made, r] = fresh
+            else:
+                thermal_out[r - rows] = fresh
+
+    @pl.loop(0, lat_count)
+    def _(step):
+        line_row = (lat + lat_count - step) % lat_count
+        direct_copy(0, line_row).wait_recv()
+
+        @pl.when(line_row % 2 == 0)
+        def _():
+            diag_copy(0, line_row).start()
+
+        chip_copy(1, line_row).start()
+        direct_copy(1, line_row).wait_recv()
+
+        @pl.when(line_row % 2 == 1)
+        def _():
+            diag_copy(1, line_row).start()
+
+        chip_copy(2, line_row).start()
+
+    @pl.loop(0, lat_count)
+    def _(step):
+        line_row = (lat + lat_count - step) % lat_count
+        diag_copy(0, line_row).wait_recv()
+        chip_copy(3, line_row).start()
+
+    own_weights.wait()
+
+    @pl.loop(1, lat_count)
+    def _(step):
+        lat_copy(step).wait_send()
+
+    @pl.loop(0, lat_count)
+    def _(line_row):
+        direct_copy(0, line_row).wait_send()
+        direct_copy(1, line_row).wait_send()
+        diag_copy(0, line_row).wait_send()
+        for which in range(4):
+            chip_copy(which, line_row).wait_send()
+
+    @pl.loop(1, groups)
+    def _(step):
+        weight_copy(step).wait()
+
+    @pl.loop(0, lat_count)
+    def _(line_row):
+        for which in range(4):
+            chip_copy(which, line_row).wait_recv()
+
+
+def fast_exchange(sizes, points, over, under, table, slots, state, weights, kappa, depth, water, ocean):
+    sec_count, lat_count, col_count = sizes
+    groups = sec_count * col_count
+    fields, width = state.shape
+    waves = table.shape[2]
+    layers, rows, span = ocean.shape
+    padded = weights.shape[1]
+    band = lat_count * padded // groups
+    chunks = width // CHUNK
+    halo_rows = rows * (layers + 4)
+    anywhere = pl.BlockSpec(memory_space=pl.ANY)
+    inside = pl.BlockSpec(memory_space=pltpu.VMEM)
+    scalar = pl.BlockSpec(memory_space=pltpu.SMEM)
+    near = len(REACH)
+    dma = pltpu.SemaphoreType.DMA
+    return pl.pallas_call(
+        functools.partial(fast_kernel, sizes),
+        out_shape=[
+            jax.ShapeDtypeStruct((groups, lat_count, padded, 2 * fields), jnp.bfloat16),
+            jax.ShapeDtypeStruct((groups, band, waves), jnp.bfloat16),
+            jax.ShapeDtypeStruct((rows, layers, span), jnp.float32),
+        ],
+        in_specs=[scalar, scalar, scalar] + [inside] * 7 + [anywhere],
+        out_specs=[inside] * 3,
+        scratch_shapes=[
+            pltpu.VMEM((groups, band, waves), jnp.bfloat16),
+            pltpu.VMEM((waves // 128, CHUNK, 256), jnp.bfloat16),
+            pltpu.VMEM((chunks * fields, CHUNK), jnp.bfloat16),
+            pltpu.VMEM((chunks * fields, 256), jnp.float32),
+            pltpu.VMEM((2 * fields, waves), jnp.bfloat16),
+            pltpu.VMEM((lat_count, padded, 2 * fields), jnp.bfloat16),
+            pltpu.VMEM((halo_rows, span), jnp.bfloat16),
+            pltpu.VMEM((halo_rows, span), jnp.bfloat16),
+            pltpu.VMEM((halo_rows, span), jnp.bfloat16),
+            pltpu.VMEM((4 * rows, span), jnp.float32),
+            pltpu.VMEM((2, 3 * rows, layers, span), jnp.float32),
+            pltpu.VMEM((3 * rows, layers, span), jnp.float32),
+            pltpu.VMEM((3 * rows, layers, span), jnp.float32),
+            pltpu.VMEM((3 * rows, layers, span), jnp.float32),
+            pltpu.VMEM((3 * rows, layers, span), jnp.float32),
+            pltpu.VMEM((2, span), jnp.float32),
+            pltpu.VMEM((near + 1, 1, span), jnp.float32),
+            dma((rows,)),
+            dma((2,)),
+            dma((groups,)),
+            dma((groups,)),
+            dma((2,)),
+            dma((2,)),
+            dma((near,)),
+            dma((near,)),
+            dma((lat_count,)),
+            dma((lat_count,)),
+            dma((2, lat_count)),
+            dma((2, lat_count)),
+            dma((lat_count,)),
+            dma((lat_count,)),
+            dma((4, lat_count)),
+            dma((4, lat_count)),
+        ],
+        compiler_params=pltpu.CompilerParams(
+            vmem_limit_bytes=48 * 2**20, collective_id=2, has_side_effects=True
+        ),
+        cost_estimate=pl.CostEstimate(
+            flops=4 * fields * waves * width, bytes_accessed=8 * 2**20, transcendentals=0
+        ),
+    )(points, over, under, table, slots, state, weights, kappa, depth, water, ocean)
+
+
+def fast_legendre_kernel(
+    degree_ref, slots_ref, weight_ref, coef_ref, ocean_ref, out_ref, ocean_out, turned_ref, ocean_sem
+):
+    groups, lines, _, width = coef_ref.shape
+    degrees = out_ref.shape[1]
+    rows = ocean_ref.shape[0]
+    halves = pl.num_programs(1)
+    major, half = pl.program_id(0), pl.program_id(1)
+    block = half * pl.num_programs(0) + major
+    copies = [
+        pltpu.make_async_copy(ocean_ref.at[r], ocean_out.at[:, r, :], ocean_sem.at[r]) for r in range(rows)
+    ]
+
+    @pl.when((major == 0) & (half == 0))
+    def _():
+        for copy in copies:
+            copy.start()
+
+    @pl.when(half == 0)
+    def _():
+        held = weight_ref[:, pl.ds(pl.multiple_of(major * 16, 16), 16), :]
+        turned_ref[...] = held.reshape(groups * 16, held.shape[2]).T
+
+    values = jnp.concatenate(
+        [
+            turned_ref[pl.ds(pl.multiple_of((t * halves + half) * degrees, 16), degrees), :]
+            for t in range(lines)
+        ],
+        axis=1,
+    )
+    cut = pl.ds(pl.multiple_of(block * 16, 16), 16)
+    coefs = jnp.concatenate(
+        [coef_ref[:, t, cut, :].reshape(groups * 16, width) for t in range(lines)], axis=0
+    )
+    odd = lax.broadcasted_iota(jnp.int32, coefs.shape, 0) % 2 == 1
+    nothing = jnp.zeros_like(coefs)
+    both = jnp.concatenate([jnp.where(odd, nothing, coefs), jnp.where(odd, coefs, nothing)], axis=1)
+    lane_pair = lax.broadcasted_iota(jnp.int32, values.shape, 1) % 16 // 2
+    left = jnp.concatenate(
+        [jnp.where(lane_pair == j, values, jnp.zeros_like(values)) for j in range(8)], axis=0
+    )
+    summed = jnp.dot(left, both, preferred_element_type=jnp.float32)
+    degree = degree_ref[0] + lax.broadcasted_iota(jnp.int32, (degrees, width), 0)
+    for s in range(16):
+        wave = slots_ref[block * 16 + s]
+        part = summed[s // 2 * degrees : (s // 2 + 1) * degrees, s % 2 * width : (s % 2 + 1) * width]
+        out_ref[s] = jnp.where(degree >= wave, part, 0.0)
+
+    @pl.when((major == pl.num_programs(0) - 1) & (half == halves - 1))
+    def _():
+        for copy in copies:
+            copy.wait()
+
+
+def fast_legendre(weights, coefs, ocean, slots, first_degree, slot_count, degrees):
+    groups, lines, padded, width = coefs.shape
+    band = weights.shape[1]
+    rows, layers, span = ocean.shape
+    halves = padded // band
+    inside = pl.BlockSpec(memory_space=pltpu.VMEM)
+    scalar = pl.BlockSpec(memory_space=pltpu.SMEM)
+    anywhere = pl.BlockSpec(memory_space=pl.ANY)
+    return pl.pallas_call(
+        fast_legendre_kernel,
+        grid=(band // 16, halves),
+        out_shape=[
+            jax.ShapeDtypeStruct((slot_count, degrees, width), jnp.float32),
+            jax.ShapeDtypeStruct((layers, rows, span), jnp.float32),
+        ],
+        in_specs=[scalar, scalar, inside, inside, anywhere],
+        out_specs=[
+            pl.BlockSpec((16, degrees, width), lambda i, h: (h * (band // 16) + i, 0, 0)),
+            anywhere,
+        ],
+        scratch_shapes=[
+            pltpu.VMEM((weights.shape[2], groups * 16), jnp.bfloat16),
+            pltpu.SemaphoreType.DMA((rows,)),
+        ],
+        compiler_params=pltpu.CompilerParams(vmem_limit_bytes=24 * 2**20),
+        cost_estimate=pl.CostEstimate(
+            flops=2 * groups * lines * padded * width * degrees * 8,
+            bytes_accessed=4 * slot_count * degrees * width,
+            transcendentals=0,
+        ),
+    )(first_degree, slots, weights, coefs, ocean)
+
+
+def fast_body(
+    physical_state,
+    parallel_lengths,
+    zonal_mode_assignment,
+    weighted_associated_polynomials,
+    marine_tracer_state,
+    lateral_diffusivity,
+    depthwise_diffusivity,
+    water_indicator,
+    overlying_parallel,
+    underlying_marine_parallel,
+):
+    sizes = tuple(lax.axis_size(name) for name in LINE)
+    sec_count, lat_count, col_count = sizes
+    groups = sec_count * col_count
+    grid_width = physical_state.shape[2]
+    slot_count, wave_count, _ = weighted_associated_polynomials.shape
+    block_degrees = wave_count // groups
+    padded = -(-slot_count // 32) * 32
+    group_index = lax.axis_index("sec") * col_count + lax.axis_index("col")
+    weights = jnp.transpose(weighted_associated_polynomials, (2, 0, 1))
+    weights = jnp.pad(weights, ((0, 0), (0, padded - slot_count), (0, 0)))
+    slots = zonal_mode_assignment.reshape(lat_count, slot_count)
+    slots = jnp.pad(slots, ((0, 0), (0, padded - slot_count)), constant_values=wave_count)
+    coefs, packed, ocean = fast_exchange(
+        sizes,
+        parallel_lengths,
+        overlying_parallel,
+        underlying_marine_parallel,
+        angle_tables(parallel_lengths[0], wave_count, grid_width),
+        slots.reshape(-1, 1),
+        physical_state[0],
+        weights,
+        lateral_diffusivity,
+        depthwise_diffusivity,
+        water_indicator,
+        marine_tracer_state,
+    )
+    own_waves = lax.dynamic_slice_in_dim(slots.reshape(-1), lax.axis_index("lat") * padded, padded)
+    first_degree = jnp.reshape(group_index * block_degrees, (1,)).astype(jnp.int32)
+    harmonic, thermal = fast_legendre(
+        packed, coefs, ocean, own_waves, first_degree, slot_count, block_degrees
+    )
+    return (jnp.transpose(harmonic, (1, 0, 2)), thermal)
+
+
+def compact(mesh):
+    return mesh.shape["sec"] == 4 and mesh.shape["lat"] == 4 and mesh.shape["col"] == 2
+
+
 def solution(mesh):
     return jax.shard_map(
-        body,
+        fast_body if compact(mesh) else body,
         mesh=mesh,
         in_specs=(
             P(LINE, None, None),

time: 95.5 us -> 57 us (0.60)
  local copies, waits for them, and re-layouts: 21.1 us -> 4.08 us
  other arithmetic: 13.4 us -> 0.87 us
  Pallas kernels: 55.3 us -> 49.6 us
  matrix products: 2.12 us -> 0 us
    unnamed x35 -> x17, local copies, waits for them, and re-layouts: 8.77 us -> 2.73 us
    pallas_call x3 -> x2, Pallas kernels: 55.3 us -> 49.6 us  [the longest x1 39.4 us: fast_exchange(): pl.pallas_call(functools.partial(fast_kernel, sizes), out_shape=[jax.Shap...]
    reshape x6 -> x3, local copies, waits for them, and re-layouts: 5.85 us -> 1.16 us  [the longest x1 0.77 us: fast_body(): slots = zonal_mode_assignment.reshape(lat_count, slot_count)]
    add x4 -> x0, other arithmetic: 4.27 us -> none  [advance_coupled_model(): return centre + meridional + zonal_div + vertical + forced]
    mul x12 -> x0, other arithmetic: 3.69 us -> none  [the longest x1 1.03 us: body(): thermal_transfer_factor * jnp.sqrt(zonal_wind * zonal_wind + meridional_w...]
    slice x30 -> x0, local copies, waits for them, and re-layouts: 3.45 us -> none  [the longest x7 1.65 us: advance_coupled_model(): east_flux = zonal_exchange_factor * (jnp.roll(centre, -1, axis=2) - centre)]
    dot_general x2 -> x0, matrix products: 2.12 us -> none  [pick_points(): jnp.einsum('kta,tx->kax', matrix, chosen, preferred_element_type=jnp.floa...]
    convert_element_type x6 -> x0, other arithmetic: 1.94 us -> none  [the longest x1 1.1 us: body(): after = jnp.where(last, jnp.zeros_like(after), after).astype(jnp.float32)]
where the time goes in v1:
time: 57 us; the launch traced here: 56.8 us
  Pallas kernels  49.6 us (87%)
  local copies, waits for them, and re-layouts  4.08 us (7%)
  between operations  2.25 us (4%)
  other arithmetic  0.87 us (2%)
    pallas_call x1, Pallas kernels, fast_exchange(): pl.pallas_call(functools.partial(fast_kernel, sizes), out_shape=[jax.Shap...  39.4 us
    pallas_call x1, Pallas kernels, fast_legendre(): pl.pallas_call(fast_legendre_kernel, grid=(band // 16, halves), out_shape...  10.2 us
    unnamed x17, local copies, waits for them, and re-layouts  2.73 us

profile of v1, /device:TPU:0, one launch (start us, length us, event | category | flops | bytes accessed | tf_op | source)
XLA Modules:
  0.0 56.8 jit_solution(12168000124399489366)
XLA Ops:
  0.6 0.0 copy-start.7
  2.2 0.1 pad_maximum_fusion
  2.2 0.8 %reshape.95 = s32[4,214]{1,0:T(4,128)S(1)} reshape(s32[856]{0:T(1024)} %param.12) | data formatting | bytes 6848 | tf_op jit(solution)/shard_map/reshape | solution.py:1196
  3.0 0.1 reshape.96
  3.1 0.1 dynamic_slice.3.slots_ref
  3.2 0.7 %fusion = (f32[1,60,640]{2,1,0:T(8,128)S(1)}, f32[1,60,640]{2,1,0:T(8,128)S(1)}) fusion(f32[]{:T(128)S(6)} %div.23, f32[]{:T(128)} %bitcast.1, f32[60]{0:T(128)S(1)} %pad_maximum_fusion), kind=kLoop, calls=%fused_computation.4 | loop fusion | flops 268800 | bytes 307448 | tf_op jit(solution)/shard_map/cos | solution.py:33
  3.9 0.1 maximum_multiply_fusion.table_ref
  4.0 0.3 reshape.98.slots_ref
  4.3 0.0 copy-done.7
  4.3 0.1 copy.16
  4.4 0.0 copy-start
  4.4 0.0 copy-start.1
  4.5 0.0 copy-start.2
  4.5 0.0 copy-start.3
  4.5 0.0 copy-start.4
  4.5 0.0 copy-start.5
  4.5 0.1 pad.9.weight_ref
  4.6 0.9 %copy-done = bf16[1,64,5120]{2,1,0:T(8,128)(2,1)S(1)} copy-done((bf16[1,64,5120]{2,1,0:T(8,128)(2,1)S(1)}, bf16[1,64,5120]{2,1,0:T(8,128)(2,1)}, u32[]{:S(2)}) %copy-start) | copy-done | bytes 655384
  5.5 0.2 copy-done.1
  5.7 0.0 copy-done.2
  5.7 0.0 copy-done.3
  5.7 39.4 %shard_map.113 = (bf16[8,4,224,128]{3,2,1,0:T(8,128)(2,1)}, bf16[8,112,640]{2,1,0:T(8,128)(2,1)S(1)}, f32[4,8,4096]{2,1,0:T(8,128)S(1)}) custom-call(s32[1]{0:T(128)S(6)} %copy.17.points_ref, s32[4]{0:T(128)S(1)} %copy-done.5, s32[1]{0:T(128)S(6)} %copy.18.under_ref, f32[2,60,640]{2,1,0:T(8,128)S(1)} %maximum_multiply_fusion.table_ref, ...), custom_call_target="tpu_custom_call" | custom-call | flops 838860800 | bytes 8388608 | tf_op jit(solution)/shard_map/pallas_call | solution.py:1034
  45.1 1.5 %copy-done.6 = bf16[8,4,224,128]{3,2,1,0:T(8,128)(2,1)S(1)} copy-done((bf16[8,4,224,128]{3,2,1,0:T(8,128)(2,1)S(1)}, bf16[8,4,224,128]{3,2,1,0:T(8,128)(2,1)}, u32[]{:S(2)}) %copy-start.6) | copy-done | bytes 1835032
  46.6 10.2 %shard_map.114 = (f32[214,80,128]{2,1,0:T(8,128)}, f32[8,4,4096]{2,1,0:T(4,128)}) custom-call(s32[1]{0:T(128)} %bitcast.degree_ref, s32[224]{0:T(256)S(1)} %dynamic_slice.3.slots_ref, bf16[8,112,640]{2,1,0:T(8,128)(2,1)S(1)} %get-tuple-element.7.weight_ref, bf16[8,4,224,128]{3,2,1,0:T(8,128)(2,1)S(1)} %copy-done.6, f32[4,8,4096]{2,1,0:T(8,128)S(1)} %get-tuple-element.9.ocean_ref), custom_call_target="tpu_custom_call" | custom-call | flops 1174405120 | bytes 8765440 | tf_op jit(solution)/shard_map/pallas_call | solution.py:1149
  (8 shorter events, 0.0 us)
Async XLA Ops:
  0.6 3.6 %copy-start.7 = (bf16[214,640,4]{1,2,0:T(4,128)(2,1)S(1)}, bf16[214,640,4]{1,2,0:T(4,128)(2,1)}, u32[]{:S(2)}) copy-start(bf16[214,640,4]{1,2,0:T(4,128)(2,1)} %param.13) | copy-start | bytes 3287044
  4.4 1.1 %copy-start = (bf16[1,64,5120]{2,1,0:T(8,128)(2,1)S(1)}, bf16[1,64,5120]{2,1,0:T(8,128)(2,1)}, u32[]{:S(2)}) copy-start(bf16[1,64,5120]{2,1,0:T(8,128)(2,1)} %param.10) | copy-start | bytes 1966084
  4.4 1.2 %copy-start.1 = (f32[8,4,4096]{2,1,0:T(4,128)S(1)}, f32[8,4,4096]{2,1,0:T(4,128)}, u32[]{:S(2)}) copy-start(f32[8,4,4096]{2,1,0:T(4,128)} %ocean_ref.1) | copy-start | bytes 1572868
  4.5 1.2 %copy-start.2 = (f32[4,4096]{1,0:T(4,128)S(1)}, f32[4,4096]{1,0:T(4,128)}, u32[]{:S(2)}) copy-start(f32[4,4096]{1,0:T(4,128)} %kappa_ref.1) | copy-start | bytes 196612
  4.5 1.2 %copy-start.3 = (f32[4,4096]{1,0:T(4,128)S(1)}, f32[4,4096]{1,0:T(4,128)}, u32[]{:S(2)}) copy-start(f32[4,4096]{1,0:T(4,128)} %depth_ref.1) | copy-start | bytes 196612
  4.5 1.2 %copy-start.4 = (s32[4,4096]{1,0:T(4,128)S(1)}, s32[4,4096]{1,0:T(4,128)}, u32[]{:S(2)}) copy-start(s32[4,4096]{1,0:T(4,128)} %water_ref.1) | copy-start | bytes 196612
  4.5 1.2 %copy-start.5 = (s32[4]{0:T(128)S(1)}, s32[4]{0:T(128)}, u32[]{:S(2)}) copy-start(s32[4]{0:T(128)} %over_ref.1) | copy-start | bytes 52
  45.1 1.5 %copy-start.6 = (bf16[8,4,224,128]{3,2,1,0:T(8,128)(2,1)S(1)}, bf16[8,4,224,128]{3,2,1,0:T(8,128)(2,1)}, u32[]{:S(2)}) copy-start(bf16[8,4,224,128]{3,2,1,0:T(8,128)(2,1)} %get-tuple-element.8.coef_ref) | copy-start | bytes 5505028

commit v2 on v1

--- a/solution.py
+++ b/solution.py
@@ -554,12 +554,11 @@
 
 def fast_kernel(
     sizes,
-    points_ref,
-    over_ref,
-    under_ref,
-    table_ref,
-    slots_ref,
-    x_ref,
+    points_hbm,
+    over_hbm,
+    under_hbm,
+    slots_hbm,
+    x_hbm,
     weight_ref,
     kappa_ref,
     depth_ref,
@@ -568,6 +567,13 @@
     coef_out,
     weight_out,
     thermal_out,
+    points_ref,
+    over_ref,
+    under_ref,
+    slots_ref,
+    x_ref,
+    table_ref,
+    strip_ref,
     msg_ref,
     base_ref,
     xm_ref,
@@ -585,6 +591,7 @@
     source_ref,
     local_ref,
     flux_ref,
+    input_sem,
     ocean_sem,
     local_sem,
     weight_send,
@@ -619,7 +626,19 @@
         pltpu.make_async_copy(ocean_ref.at[:, r, :], heat_ref.at[0, rows + r], ocean_sem.at[r])
         for r in range(rows)
     ]
-    for copy in ocean_copies:
+    inputs = [
+        pltpu.make_async_copy(source, target, input_sem.at[k])
+        for k, (source, target) in enumerate(
+            (
+                (points_hbm, points_ref),
+                (over_hbm, over_ref),
+                (under_hbm, under_ref),
+                (slots_hbm, slots_ref),
+                (x_hbm, x_ref),
+            )
+        )
+    ]
+    for copy in ocean_copies + inputs:
         copy.start()
 
     def group_place(step):
@@ -738,21 +757,24 @@
     own_weights = pltpu.make_async_copy(msg_ref.at[group], weight_out.at[group], local_sem.at[0])
     own_weights.start()
 
+    for copy in inputs[:-1] + ocean_copies:
+        copy.wait()
     sea = water_ref[...].astype(jnp.float32)
-    plane_ref[0:rows] = kappa_ref[...] * sea
-    plane_ref[rows : 2 * rows] = depth_ref[...] * sea
-    row_index = lax.broadcasted_iota(jnp.int32, (rows, span), 0)
-    relative = jnp.zeros((rows, span), jnp.float32)
-    for r in range(rows):
-        relative = jnp.where(row_index == r, (over_ref[r] - line).astype(jnp.float32), relative)
-    plane_ref[2 * rows : 3 * rows] = relative
-    plane_ref[3 * rows : 4 * rows] = relative
-    halo_ref[rows * layers :] = plane_ref[...].astype(jnp.bfloat16)
-    for copy in ocean_copies:
-        copy.wait()
-    for r in range(0, rows, 2):
-        pair = jnp.concatenate([heat_ref[0, rows + r], heat_ref[0, rows + r + 1]], axis=0)
-        halo_ref[r * layers : (r + 2) * layers] = pair.astype(jnp.bfloat16)
+    plane_ref[:rows] = kappa_ref[...] * sea
+    plane_ref[rows:] = depth_ref[...] * sea
+    deep = rows * layers
+    part = span // 2
+    for side in range(2):
+        cut = slice(side * part, side * part + part)
+        for r in range(0, rows, 2):
+            pair = jnp.concatenate(
+                [heat_ref[0, rows + r, :, cut], heat_ref[0, rows + r + 1, :, cut]], axis=0
+            )
+            first = side * deep + r * layers
+            halo_ref[first : first + 2 * layers] = pair.astype(jnp.bfloat16)
+    halo_ref[2 * deep :] = jnp.concatenate(
+        [plane_ref[:, :part], plane_ref[:, part:]], axis=0
+    ).astype(jnp.bfloat16)
 
     @pl.when(has_next)
     def _():
@@ -766,6 +788,18 @@
     waves = table_ref.shape[2]
     fields = x_ref.shape[0]
     chunks = x_ref.shape[1] // CHUNK
+    top = LOW + CHUNK // LOW
+    shape = table_ref.shape[1:]
+    place = lax.broadcasted_iota(jnp.int32, shape, 0)
+    place = jnp.where(
+        place < LOW, place, jnp.where(place < top, (place - LOW) * LOW, (place - top) * CHUNK)
+    )
+    product = place.astype(jnp.float32) * lax.broadcasted_iota(jnp.int32, shape, 1).astype(jnp.float32)
+    count = jnp.full(shape, points, jnp.int32).astype(jnp.float32)
+    angle = (product - jnp.round(product / count) * count) * (two_pi / count)
+    scale = jnp.where(lax.broadcasted_iota(jnp.int32, shape, 0) >= top, 1.0 / jnp.sqrt(count), 1.0)
+    table_ref[0] = jnp.cos(angle) * scale
+    table_ref[1] = -jnp.sin(angle) * scale
     low_c, low_s = table_ref[0, :LOW], table_ref[1, :LOW]
     for w in range(waves // 128):
         cut = slice(w * 128, w * 128 + 128)
@@ -780,13 +814,13 @@
             imag = jnp.concatenate(imag, axis=0).astype(jnp.bfloat16)
             base_ref[w, b * LOW : (b + 2) * LOW, :128] = real
             base_ref[w, b * LOW : (b + 2) * LOW, 128:] = imag
+    inputs[-1].wait()
     for a in range(chunks):
         position = a * CHUNK + lax.broadcasted_iota(jnp.int32, (fields, CHUNK), 1)
         block = x_ref[:, a * CHUNK : (a + 1) * CHUNK].astype(jnp.float32)
         xm_ref[a * fields : (a + 1) * fields] = jnp.where(position < points, block, 0.0).astype(
             jnp.bfloat16
         )
-    top = LOW + CHUNK // LOW
     for w in range(waves // 128):
         cut = slice(w * 128, w * 128 + 128)
         z_ref[...] = jnp.dot(xm_ref[...], base_ref[w], preferred_element_type=jnp.float32)
@@ -805,13 +839,20 @@
         coefs_ref[fields:, cut] = jnp.where(kept, imag, 0.0).astype(jnp.bfloat16)
     padded = mine_ref.shape[1]
 
+    slot_total = slots_ref.shape[0]
+    slot_count = slot_total // lat_count
+    ring = strip_ref.shape[1]
+    lanes = -(-padded // 128) * 128
+    strip_ref[...] = jnp.full_like(strip_ref, waves)
+    strip_ref[0:1, :slot_total] = slots_ref[...].reshape(1, slot_total)
+
     def fill(other):
-        held = slots_ref[pl.ds(pl.multiple_of(other * padded, 16), padded)]
-        pick = held == lax.broadcasted_iota(jnp.int32, (padded, waves), 1)
+        held = pltpu.roll(strip_ref[...], ring - other * slot_count, 1)[0:1, :lanes]
+        held = jnp.where(lax.broadcasted_iota(jnp.int32, (1, lanes), 1) < slot_count, held, waves)
+        pick = held == lax.broadcasted_iota(jnp.int32, (waves, lanes), 0)
         pick = jnp.where(pick, 1.0, 0.0).astype(jnp.bfloat16)
-        mine_ref[other] = lax.dot_general(
-            pick, coefs_ref[...], (((1,), (1,)), ((), ())), preferred_element_type=jnp.float32
-        ).astype(jnp.bfloat16)
+        chosen = jnp.dot(coefs_ref[...], pick, preferred_element_type=jnp.float32)
+        mine_ref[other] = chosen.T[:padded].astype(jnp.bfloat16)
 
     @pl.loop(1, lat_count)
     def _(step):
@@ -889,11 +930,14 @@
     def _():
         before_ref[...] = jnp.zeros_like(before_ref)
 
-    for r in range(0, rows, 2):
-        for start, held in ((0, before_ref), (2 * rows, after_ref)):
-            pair = held[r * layers : (r + 2) * layers].astype(jnp.float32)
-            heat_ref[0, start + r] = pair[:layers]
-            heat_ref[0, start + r + 1] = pair[layers:]
+    for start, held in ((0, before_ref), (2 * rows, after_ref)):
+        for side in range(2):
+            for r in range(0, rows, 2):
+                first = side * deep + r * layers
+                pair = held[first : first + 2 * layers].astype(jnp.float32)
+                cut = slice(side * part, side * part + part)
+                heat_ref[0, start + r, :, cut] = pair[:layers]
+                heat_ref[0, start + r + 1, :, cut] = pair[layers:]
 
     under = under_ref[0] - (line - 1) * rows
     skin = jnp.zeros((1, span), jnp.float32)
@@ -914,6 +958,11 @@
         cut = pl.ds(start, wide)
         flux_ref[len(REACH), 0:1, cut] = local_ref[0:1, cut] * (upper + lower - local_ref[1:2, cut])
 
+    lane = lax.broadcasted_iota(jnp.int32, (1, 128), 1)
+    relative = jnp.zeros((1, 128), jnp.float32)
+    for r in range(rows):
+        relative = jnp.where(lane == r, (over_ref[r] - line).astype(jnp.float32), relative)
+    flux_ref[len(REACH), 0:1, span:] = relative
     for k in range(len(REACH)):
         flux_copy(k).start()
 
@@ -922,14 +971,12 @@
         lat_copy(step).wait_recv()
         spread_piece((lat + lat_count - step) % lat_count)
 
-    edges = [before_ref[rows * layers :].astype(jnp.float32), after_ref[rows * layers :].astype(jnp.float32)]
-    centre = plane_ref[...]
-    kappa = jnp.concatenate([edges[0][:rows], centre[:rows], edges[1][:rows]], axis=0)
-    depth = jnp.concatenate([edges[0][rows : 2 * rows], centre[rows : 2 * rows], edges[1][rows : 2 * rows]], axis=0)
-    reach = jnp.concatenate(
-        [edges[0][2 * rows : 3 * rows] - 1.0, centre[2 * rows : 3 * rows], edges[1][2 * rows : 3 * rows] + 1.0],
-        axis=0,
-    )
+    edges = []
+    for held in (before_ref, after_ref):
+        coarse = held[2 * deep :].astype(jnp.float32)
+        edges.append(jnp.concatenate([coarse[: 2 * rows], coarse[2 * rows :]], axis=1))
+    kappa = jnp.concatenate([edges[0][:rows], plane_ref[:rows], edges[1][:rows]], axis=0)
+    depth = jnp.concatenate([edges[0][rows:], plane_ref[rows:], edges[1][rows:]], axis=0)
     total = 3 * rows
     layer = lax.broadcasted_iota(jnp.int32, (layers, span), 0)
     beside = pltpu.roll(kappa, span - 1, 1)
@@ -944,14 +991,17 @@
 
     for k in range(len(REACH)):
         flux_copy(k).wait()
-    forcing = jnp.zeros_like(kappa)
-    for k, step in enumerate(REACH + (0,)):
-        forcing = jnp.where(reach == float(step), flux_ref[k], forcing)
-    forcing = jnp.where(kappa > 0.0, force_coef * forcing, 0.0)
+    near = REACH + (0,)
     for r in range(1, total - 1):
-        source_ref[r] = jnp.where(layer == 0, forcing[r : r + 1], 0.0)
-
-    for step in range(OSTEPS):
+        owner = r // rows - 1
+        target = flux_ref[near.index(owner), 0:1, span + r % rows : span + r % rows + 1] + float(owner)
+        row = jnp.zeros((1, span), jnp.float32)
+        for k, step in enumerate(near):
+            row = jnp.where(target == float(step), flux_ref[k, 0:1, :span], row)
+        row = jnp.where(kappa[r : r + 1] > 0.0, force_coef * row, 0.0)
+        source_ref[r] = jnp.where(layer == 0, row, 0.0)
+
+    def ocean_step(step):
         held, made = step % 2, (step + 1) % 2
 
         @pl.loop(step + 1, total - step - 1)
@@ -968,6 +1018,9 @@
             else:
                 thermal_out[r - rows] = fresh
 
+    ocean_step(0)
+    ocean_step(1)
+
     @pl.loop(0, lat_count)
     def _(step):
         line_row = (lat + lat_count - step) % lat_count
@@ -985,6 +1038,9 @@
             diag_copy(1, line_row).start()
 
         chip_copy(2, line_row).start()
+
+    ocean_step(2)
+    ocean_step(3)
 
     @pl.loop(0, lat_count)
     def _(step):
@@ -1016,19 +1072,19 @@
             chip_copy(which, line_row).wait_recv()
 
 
-def fast_exchange(sizes, points, over, under, table, slots, state, weights, kappa, depth, water, ocean):
+def fast_exchange(sizes, points, over, under, slots, state, weights, kappa, depth, water, ocean):
     sec_count, lat_count, col_count = sizes
     groups = sec_count * col_count
     fields, width = state.shape
-    waves = table.shape[2]
+    waves = weights.shape[2]
+    table_rows = -(-(LOW + CHUNK // LOW + width // CHUNK) // 8) * 8
     layers, rows, span = ocean.shape
     padded = weights.shape[1]
     band = lat_count * padded // groups
     chunks = width // CHUNK
-    halo_rows = rows * (layers + 4)
-    anywhere = pl.BlockSpec(memory_space=pl.ANY)
+    halo_rows = 2 * rows * (layers + 2)
     inside = pl.BlockSpec(memory_space=pltpu.VMEM)
-    scalar = pl.BlockSpec(memory_space=pltpu.SMEM)
+    outside = pl.BlockSpec(memory_space=pl.ANY)
     near = len(REACH)
     dma = pltpu.SemaphoreType.DMA
     return pl.pallas_call(
@@ -1038,26 +1094,34 @@
             jax.ShapeDtypeStruct((groups, band, waves), jnp.bfloat16),
             jax.ShapeDtypeStruct((rows, layers, span), jnp.float32),
         ],
-        in_specs=[scalar, scalar, scalar] + [inside] * 7 + [anywhere],
+        in_specs=[outside] * 5 + [inside] * 4 + [outside],
         out_specs=[inside] * 3,
         scratch_shapes=[
+            pltpu.SMEM(points.shape, jnp.int32),
+            pltpu.SMEM(over.shape, jnp.int32),
+            pltpu.SMEM(under.shape, jnp.int32),
+            pltpu.VMEM(slots.shape, jnp.int32),
+            pltpu.VMEM(state.shape, state.dtype),
+            pltpu.VMEM((2, table_rows, waves), jnp.float32),
+            pltpu.VMEM((8, -(-(slots.shape[0] + 256) // 128) * 128), jnp.int32),
             pltpu.VMEM((groups, band, waves), jnp.bfloat16),
             pltpu.VMEM((waves // 128, CHUNK, 256), jnp.bfloat16),
             pltpu.VMEM((chunks * fields, CHUNK), jnp.bfloat16),
             pltpu.VMEM((chunks * fields, 256), jnp.float32),
             pltpu.VMEM((2 * fields, waves), jnp.bfloat16),
             pltpu.VMEM((lat_count, padded, 2 * fields), jnp.bfloat16),
-            pltpu.VMEM((halo_rows, span), jnp.bfloat16),
-            pltpu.VMEM((halo_rows, span), jnp.bfloat16),
-            pltpu.VMEM((halo_rows, span), jnp.bfloat16),
-            pltpu.VMEM((4 * rows, span), jnp.float32),
+            pltpu.VMEM((halo_rows, span // 2), jnp.bfloat16),
+            pltpu.VMEM((halo_rows, span // 2), jnp.bfloat16),
+            pltpu.VMEM((halo_rows, span // 2), jnp.bfloat16),
+            pltpu.VMEM((2 * rows, span), jnp.float32),
             pltpu.VMEM((2, 3 * rows, layers, span), jnp.float32),
             pltpu.VMEM((3 * rows, layers, span), jnp.float32),
             pltpu.VMEM((3 * rows, layers, span), jnp.float32),
             pltpu.VMEM((3 * rows, layers, span), jnp.float32),
             pltpu.VMEM((3 * rows, layers, span), jnp.float32),
             pltpu.VMEM((2, span), jnp.float32),
-            pltpu.VMEM((near + 1, 1, span), jnp.float32),
+            pltpu.VMEM((near + 1, 1, span + 128), jnp.float32),
+            dma((5,)),
             dma((rows,)),
             dma((2,)),
             dma((groups,)),
@@ -1076,99 +1140,135 @@
             dma((4, lat_count)),
         ],
         compiler_params=pltpu.CompilerParams(
-            vmem_limit_bytes=48 * 2**20, collective_id=2, has_side_effects=True
+            vmem_limit_bytes=28 * 2**20, collective_id=2, has_side_effects=True
         ),
         cost_estimate=pl.CostEstimate(
             flops=4 * fields * waves * width, bytes_accessed=8 * 2**20, transcendentals=0
         ),
-    )(points, over, under, table, slots, state, weights, kappa, depth, water, ocean)
+    )(points, over, under, slots, state, weights, kappa, depth, water, ocean)
 
 
 def fast_legendre_kernel(
-    degree_ref, slots_ref, weight_ref, coef_ref, ocean_ref, out_ref, ocean_out, turned_ref, ocean_sem
+    col_count,
+    slots_hbm,
+    weight_ref,
+    coef_ref,
+    ocean_ref,
+    out_ref,
+    ocean_out,
+    slots_ref,
+    turned_ref,
+    made_ref,
+    made_sem,
+    ocean_sem,
+    slots_sem,
 ):
-    groups, lines, _, width = coef_ref.shape
-    degrees = out_ref.shape[1]
+    groups, lines, padded, width = coef_ref.shape
+    slot_count, degrees, _ = out_ref.shape
     rows = ocean_ref.shape[0]
-    halves = pl.num_programs(1)
-    major, half = pl.program_id(0), pl.program_id(1)
-    block = half * pl.num_programs(0) + major
-    copies = [
+    blocks = padded // 16
+    rest = slot_count - (blocks - 1) * 16
+    halves = padded // weight_ref.shape[1]
+    majors = blocks // halves
+    ocean_copies = [
         pltpu.make_async_copy(ocean_ref.at[r], ocean_out.at[:, r, :], ocean_sem.at[r]) for r in range(rows)
     ]
-
-    @pl.when((major == 0) & (half == 0))
-    def _():
-        for copy in copies:
-            copy.start()
-
-    @pl.when(half == 0)
-    def _():
+    slots_copy = pltpu.make_async_copy(slots_hbm, slots_ref, slots_sem)
+    slots_copy.start()
+    for copy in ocean_copies:
+        copy.start()
+    first_slot = lax.axis_index("lat") * slot_count
+    last_slot = slots_ref.shape[0] - 1
+    first_degree = (lax.axis_index("sec") * col_count + lax.axis_index("col")) * degrees
+
+    def made_copy(block, count):
+        cut = pl.ds(block * 16, count)
+        return pltpu.make_async_copy(made_ref.at[cut], out_ref.at[cut], made_sem.at[block])
+
+    degree = first_degree + lax.broadcasted_iota(jnp.int32, (degrees, width), 0)
+    odd = lax.broadcasted_iota(jnp.int32, (lines * groups * 16, width), 0) % 2 == 1
+    lane_pair = lax.broadcasted_iota(jnp.int32, (degrees, lines * groups * 16), 1) % 16 // 2
+
+    slots_copy.wait()
+
+    @pl.loop(0, majors)
+    def _(major):
         held = weight_ref[:, pl.ds(pl.multiple_of(major * 16, 16), 16), :]
         turned_ref[...] = held.reshape(groups * 16, held.shape[2]).T
-
-    values = jnp.concatenate(
-        [
-            turned_ref[pl.ds(pl.multiple_of((t * halves + half) * degrees, 16), degrees), :]
-            for t in range(lines)
-        ],
-        axis=1,
-    )
-    cut = pl.ds(pl.multiple_of(block * 16, 16), 16)
-    coefs = jnp.concatenate(
-        [coef_ref[:, t, cut, :].reshape(groups * 16, width) for t in range(lines)], axis=0
-    )
-    odd = lax.broadcasted_iota(jnp.int32, coefs.shape, 0) % 2 == 1
-    nothing = jnp.zeros_like(coefs)
-    both = jnp.concatenate([jnp.where(odd, nothing, coefs), jnp.where(odd, coefs, nothing)], axis=1)
-    lane_pair = lax.broadcasted_iota(jnp.int32, values.shape, 1) % 16 // 2
-    left = jnp.concatenate(
-        [jnp.where(lane_pair == j, values, jnp.zeros_like(values)) for j in range(8)], axis=0
-    )
-    summed = jnp.dot(left, both, preferred_element_type=jnp.float32)
-    degree = degree_ref[0] + lax.broadcasted_iota(jnp.int32, (degrees, width), 0)
-    for s in range(16):
-        wave = slots_ref[block * 16 + s]
-        part = summed[s // 2 * degrees : (s // 2 + 1) * degrees, s % 2 * width : (s % 2 + 1) * width]
-        out_ref[s] = jnp.where(degree >= wave, part, 0.0)
-
-    @pl.when((major == pl.num_programs(0) - 1) & (half == halves - 1))
-    def _():
-        for copy in copies:
-            copy.wait()
-
-
-def fast_legendre(weights, coefs, ocean, slots, first_degree, slot_count, degrees):
+        for half in range(halves):
+            block = half * majors + major
+            values = jnp.concatenate(
+                [
+                    turned_ref[(t * halves + half) * degrees : (t * halves + half + 1) * degrees, :]
+                    for t in range(lines)
+                ],
+                axis=1,
+            )
+            cut = pl.ds(pl.multiple_of(block * 16, 16), 16)
+            coefs = jnp.concatenate(
+                [coef_ref[:, t, cut, :].reshape(groups * 16, width) for t in range(lines)], axis=0
+            )
+            nothing = jnp.zeros_like(coefs)
+            both = jnp.concatenate(
+                [jnp.where(odd, nothing, coefs), jnp.where(odd, coefs, nothing)], axis=1
+            )
+            left = jnp.concatenate(
+                [jnp.where(lane_pair == j, values, jnp.zeros_like(values)) for j in range(8)], axis=0
+            )
+            summed = jnp.dot(left, both, preferred_element_type=jnp.float32)
+            for s in range(16):
+                wave = slots_ref[jnp.minimum(first_slot + block * 16 + s, last_slot)]
+                part = summed[
+                    s // 2 * degrees : (s // 2 + 1) * degrees, s % 2 * width : (s % 2 + 1) * width
+                ]
+                made_ref[block * 16 + s] = jnp.where(degree >= wave, part, 0.0)
+
+            @pl.when(block < blocks - 1)
+            def _():
+                made_copy(block, 16).start()
+
+            @pl.when(block == blocks - 1)
+            def _():
+                made_copy(block, rest).start()
+
+    @pl.loop(0, blocks - 1)
+    def _(block):
+        made_copy(block, 16).wait()
+
+    made_copy(blocks - 1, rest).wait()
+    for copy in ocean_copies:
+        copy.wait()
+
+
+def fast_legendre(col_count, weights, coefs, ocean, slots, slot_count, degrees):
     groups, lines, padded, width = coefs.shape
-    band = weights.shape[1]
     rows, layers, span = ocean.shape
-    halves = padded // band
     inside = pl.BlockSpec(memory_space=pltpu.VMEM)
-    scalar = pl.BlockSpec(memory_space=pltpu.SMEM)
+    outside = pl.BlockSpec(memory_space=pl.ANY)
     anywhere = pl.BlockSpec(memory_space=pl.ANY)
     return pl.pallas_call(
-        fast_legendre_kernel,
-        grid=(band // 16, halves),
+        functools.partial(fast_legendre_kernel, col_count),
         out_shape=[
             jax.ShapeDtypeStruct((slot_count, degrees, width), jnp.float32),
             jax.ShapeDtypeStruct((layers, rows, span), jnp.float32),
         ],
-        in_specs=[scalar, scalar, inside, inside, anywhere],
-        out_specs=[
-            pl.BlockSpec((16, degrees, width), lambda i, h: (h * (band // 16) + i, 0, 0)),
-            anywhere,
+        in_specs=[outside, inside, inside, inside],
+        out_specs=[anywhere, anywhere],
+        scratch_shapes=[
+            pltpu.SMEM(slots.shape, jnp.int32),
+            pltpu.VMEM((weights.shape[2], groups * 16), jnp.bfloat16),
+            pltpu.VMEM((padded, degrees, width), jnp.float32),
+            pltpu.SemaphoreType.DMA((padded // 16,)),
+            pltpu.SemaphoreType.DMA((rows,)),
+            pltpu.SemaphoreType.DMA,
         ],
-        scratch_shapes=[
-            pltpu.VMEM((weights.shape[2], groups * 16), jnp.bfloat16),
-            pltpu.SemaphoreType.DMA((rows,)),
-        ],
-        compiler_params=pltpu.CompilerParams(vmem_limit_bytes=24 * 2**20),
+        compiler_params=pltpu.CompilerParams(vmem_limit_bytes=32 * 2**20),
         cost_estimate=pl.CostEstimate(
             flops=2 * groups * lines * padded * width * degrees * 8,
             bytes_accessed=4 * slot_count * degrees * width,
             transcendentals=0,
         ),
-    )(first_degree, slots, weights, coefs, ocean)
+    )(slots, weights, coefs, ocean)
 
 
 def fast_body(
@@ -1186,22 +1286,17 @@
     sizes = tuple(lax.axis_size(name) for name in LINE)
     sec_count, lat_count, col_count = sizes
     groups = sec_count * col_count
-    grid_width = physical_state.shape[2]
     slot_count, wave_count, _ = weighted_associated_polynomials.shape
     block_degrees = wave_count // groups
     padded = -(-slot_count // 32) * 32
-    group_index = lax.axis_index("sec") * col_count + lax.axis_index("col")
     weights = jnp.transpose(weighted_associated_polynomials, (2, 0, 1))
     weights = jnp.pad(weights, ((0, 0), (0, padded - slot_count), (0, 0)))
-    slots = zonal_mode_assignment.reshape(lat_count, slot_count)
-    slots = jnp.pad(slots, ((0, 0), (0, padded - slot_count)), constant_values=wave_count)
     coefs, packed, ocean = fast_exchange(
         sizes,
         parallel_lengths,
         overlying_parallel,
         underlying_marine_parallel,
-        angle_tables(parallel_lengths[0], wave_count, grid_width),
-        slots.reshape(-1, 1),
+        zonal_mode_assignment,
         physical_state[0],
         weights,
         lateral_diffusivity,
@@ -1209,10 +1304,8 @@
         water_indicator,
         marine_tracer_state,
     )
-    own_waves = lax.dynamic_slice_in_dim(slots.reshape(-1), lax.axis_index("lat") * padded, padded)
-    first_degree = jnp.reshape(group_index * block_degrees, (1,)).astype(jnp.int32)
     harmonic, thermal = fast_legendre(
-        packed, coefs, ocean, own_waves, first_degree, slot_count, block_degrees
+        col_count, packed, coefs, ocean, zonal_mode_assignment, slot_count, block_degrees
     )
     return (jnp.transpose(harmonic, (1, 0, 2)), thermal)
 

time: 57 us -> 46.8 us (0.82)
  Pallas kernels: 49.6 us -> 42.1 us
  local copies, waits for them, and re-layouts: 4.08 us -> 2.57 us
  other arithmetic: 0.87 us -> 0 us
    pallas_call x1, Pallas kernels: 10.2 us -> 5.82 us  [fast_legendre(): pl.pallas_call(functools.partial(fast_legendre_kernel, col_count), out_sh...]
    pallas_call x1, Pallas kernels: 39.4 us -> 36.2 us  [fast_exchange(): pl.pallas_call(functools.partial(fast_kernel, sizes), out_shape=[jax.Shap...]
    reshape x3 -> x0, local copies, waits for them, and re-layouts: 1.16 us -> none  [the longest x1 0.77 us: fast_body(): slots = zonal_mode_assignment.reshape(lat_count, slot_count)]
    cos x1 -> x0, other arithmetic: 0.69 us -> none  [angle_tables(): return jnp.stack([jnp.cos(angle), -jnp.sin(angle)]) * scale[None, :, None]]
    unnamed x17 -> x15, local copies, waits for them, and re-layouts: 2.73 us -> 2.47 us
where the time goes in v2:
time: 46.8 us; the launch traced here: 46.6 us
  Pallas kernels  42.1 us (90%)
  local copies, waits for them, and re-layouts  2.57 us (5%)
  between operations  2.01 us (4%)
    pallas_call x1, Pallas kernels, fast_exchange(): pl.pallas_call(functools.partial(fast_kernel, sizes), out_shape=[jax.Shap...  36.2 us
    pallas_call x1, Pallas kernels, fast_legendre(): pl.pallas_call(functools.partial(fast_legendre_kernel, col_count), out_sh...  5.82 us
    unnamed x15, local copies, waits for them, and re-layouts  2.47 us

profile of v2, /device:TPU:0, one launch (start us, length us, event | category | flops | bytes accessed | tf_op | source)
XLA Modules:
  0.0 46.6 jit_solution(283366774828936261)
XLA Ops:
  1.9 1.4 %copy.14 = bf16[214,640,4]{1,0,2:T(8,128)(2,1)S(1)} copy(bf16[214,640,4]{1,2,0:T(4,128)(2,1)} %param.13) | data formatting | bytes 2191360 | tf_op args[3]
  3.3 0.0 copy-start
  3.3 0.0 copy-start.1
  3.3 0.0 copy-start.2
  3.3 0.0 copy-start.3
  3.4 0.0 copy-start.4
  3.4 0.0 copy-start.5
  3.4 0.0 copy-start.6
  3.4 0.1 pad.4.weight_ref
  3.5 0.9 %copy-done = bf16[1,64,5120]{2,1,0:T(8,128)(2,1)S(1)} copy-done((bf16[1,64,5120]{2,1,0:T(8,128)(2,1)S(1)}, bf16[1,64,5120]{2,1,0:T(8,128)(2,1)}, u32[]{:S(2)}) %copy-start) | copy-done | bytes 655384
  4.4 0.2 copy-done.1
  4.5 0.0 copy-done.2
  4.5 0.0 copy-done.3
  4.6 0.0 copy-done.4
  4.6 0.0 copy-done.5
  4.6 0.0 copy-done.6
  4.6 36.2 %shard_map.113 = (bf16[8,4,224,128]{3,2,1,0:T(8,128)(2,1)S(1)}, bf16[8,112,640]{2,1,0:T(8,128)(2,1)S(1)}, f32[4,8,4096]{2,1,0:T(8,128)S(1)}) custom-call(s32[1]{0:T(128)S(6)} %copy.15.points_hbm, s32[4]{0:T(128)S(1)} %copy-done.6, s32[1]{0:T(128)S(6)} %copy.16.under_hbm, s32[856]{0:T(1024)S(1)} %copy-done.5, bf16[64,5120]{1,0:T(8,128)(2,1)S(1)} %bitcast.5, ...), custom_call_target="tpu_custom_call" | custom-call | flops 838860800 | bytes 8388608 | tf_op jit(solution)/shard_map/pallas_call | solution.py:1090
  40.8 5.8 %shard_map.114 = (f32[214,80,128]{2,1,0:T(8,128)}, f32[8,4,4096]{2,1,0:T(4,128)}) custom-call(s32[856]{0:T(1024)S(1)} %copy-done.5, bf16[8,112,640]{2,1,0:T(8,128)(2,1)S(1)} %get-tuple-element.7.weight_ref, bf16[8,4,224,128]{3,2,1,0:T(8,128)(2,1)S(1)} %get-tuple-element.8.coef_ref, f32[4,8,4096]{2,1,0:T(8,128)S(1)} %get-tuple-element.9.ocean_ref), custom_call_target="tpu_custom_call" | custom-call | flops 1174405120 | bytes 8765440 | tf_op jit(solution)/shard_map/pallas_call | solution.py:1249
Async XLA Ops:
  3.3 1.1 %copy-start = (bf16[1,64,5120]{2,1,0:T(8,128)(2,1)S(1)}, bf16[1,64,5120]{2,1,0:T(8,128)(2,1)}, u32[]{:S(2)}) copy-start(bf16[1,64,5120]{2,1,0:T(8,128)(2,1)} %param.10) | copy-start | bytes 1966084
  3.3 1.2 %copy-start.1 = (f32[8,4,4096]{2,1,0:T(4,128)S(1)}, f32[8,4,4096]{2,1,0:T(4,128)}, u32[]{:S(2)}) copy-start(f32[8,4,4096]{2,1,0:T(4,128)} %ocean_ref.1) | copy-start | bytes 1572868
  3.3 1.2 %copy-start.2 = (f32[4,4096]{1,0:T(4,128)S(1)}, f32[4,4096]{1,0:T(4,128)}, u32[]{:S(2)}) copy-start(f32[4,4096]{1,0:T(4,128)} %kappa_ref.1) | copy-start | bytes 196612
  3.3 1.2 %copy-start.3 = (f32[4,4096]{1,0:T(4,128)S(1)}, f32[4,4096]{1,0:T(4,128)}, u32[]{:S(2)}) copy-start(f32[4,4096]{1,0:T(4,128)} %depth_ref.1) | copy-start | bytes 196612
  3.4 1.2 %copy-start.4 = (s32[4,4096]{1,0:T(4,128)S(1)}, s32[4,4096]{1,0:T(4,128)}, u32[]{:S(2)}) copy-start(s32[4,4096]{1,0:T(4,128)} %water_ref.1) | copy-start | bytes 196612
  3.4 1.2 %copy-start.5 = (s32[856]{0:T(1024)S(1)}, s32[856]{0:T(1024)}, u32[]{:S(2)}) copy-start(s32[856]{0:T(1024)} %slots_hbm.3) | copy-start | bytes 10276
  3.4 1.2 %copy-start.6 = (s32[4]{0:T(128)S(1)}, s32[4]{0:T(128)}, u32[]{:S(2)}) copy-start(s32[4]{0:T(128)} %over_hbm.1) | copy-start | bytes 52

commit v3 on v2

--- a/solution.py
+++ b/solution.py
@@ -642,7 +642,10 @@
         copy.start()
 
     def group_place(step):
-        other = (group + step) % groups
+        bit0 = (group % 2 + step % 2) % 2
+        bit1 = (group // 2 % 2 + step // 2 % 2) % 2
+        bit2 = (group // 4 + step // 4) % 2
+        other = 4 * bit2 + 2 * bit1 + bit0
         return other, {"sec": other // col_count, "lat": lat, "col": other % col_count}
 
     def lat_place(step):
@@ -747,15 +750,6 @@
             msg_ref[g, :, p * degrees : (p + 1) * degrees] = weight_ref[
                 t, h * band : (h + 1) * band, g * degrees : (g + 1) * degrees
             ]
-
-    pl.semaphore_wait(barrier, len(REACH) + groups - 1 + lat_count - 1)
-
-    @pl.loop(1, groups)
-    def _(step):
-        weight_copy(step).start()
-
-    own_weights = pltpu.make_async_copy(msg_ref.at[group], weight_out.at[group], local_sem.at[0])
-    own_weights.start()
 
     for copy in inputs[:-1] + ocean_copies:
         copy.wait()
@@ -776,6 +770,8 @@
         [plane_ref[:, :part], plane_ref[:, part:]], axis=0
     ).astype(jnp.bfloat16)
 
+    pl.semaphore_wait(barrier, len(REACH) + groups - 1 + lat_count - 1)
+
     @pl.when(has_next)
     def _():
         halo_copy(0).start()
@@ -783,6 +779,13 @@
     @pl.when(has_previous)
     def _():
         halo_copy(1).start()
+
+    @pl.loop(1, 7)
+    def _(step):
+        weight_copy(step).start()
+
+    own_weights = pltpu.make_async_copy(msg_ref.at[group], weight_out.at[group], local_sem.at[0])
+    own_weights.start()
 
     points = points_ref[0]
     waves = table_ref.shape[2]
@@ -970,6 +973,8 @@
     def _(step):
         lat_copy(step).wait_recv()
         spread_piece((lat + lat_count - step) % lat_count)
+
+    weight_copy(7).start()
 
     edges = []
     for held in (before_ref, after_ref):
@@ -1191,20 +1196,19 @@
 
     slots_copy.wait()
 
-    @pl.loop(0, majors)
-    def _(major):
-        held = weight_ref[:, pl.ds(pl.multiple_of(major * 16, 16), 16), :]
-        turned_ref[...] = held.reshape(groups * 16, held.shape[2]).T
+    for major in range(majors):
+        held = weight_ref[:, major * 16 : major * 16 + 16, :]
+        turned_ref[major % 2] = held.reshape(groups * 16, held.shape[2]).T
         for half in range(halves):
             block = half * majors + major
             values = jnp.concatenate(
                 [
-                    turned_ref[(t * halves + half) * degrees : (t * halves + half + 1) * degrees, :]
+                    turned_ref[major % 2, (t * halves + half) * degrees : (t * halves + half + 1) * degrees, :]
                     for t in range(lines)
                 ],
                 axis=1,
             )
-            cut = pl.ds(pl.multiple_of(block * 16, 16), 16)
+            cut = slice(block * 16, block * 16 + 16)
             coefs = jnp.concatenate(
                 [coef_ref[:, t, cut, :].reshape(groups * 16, width) for t in range(lines)], axis=0
             )
@@ -1223,13 +1227,7 @@
                 ]
                 made_ref[block * 16 + s] = jnp.where(degree >= wave, part, 0.0)
 
-            @pl.when(block < blocks - 1)
-            def _():
-                made_copy(block, 16).start()
-
-            @pl.when(block == blocks - 1)
-            def _():
-                made_copy(block, rest).start()
+            made_copy(block, 16 if block < blocks - 1 else rest).start()
 
     @pl.loop(0, blocks - 1)
     def _(block):
@@ -1256,7 +1254,7 @@
         out_specs=[anywhere, anywhere],
         scratch_shapes=[
             pltpu.SMEM(slots.shape, jnp.int32),
-            pltpu.VMEM((weights.shape[2], groups * 16), jnp.bfloat16),
+            pltpu.VMEM((2, weights.shape[2], groups * 16), jnp.bfloat16),
             pltpu.VMEM((padded, degrees, width), jnp.float32),
             pltpu.SemaphoreType.DMA((padded // 16,)),
             pltpu.SemaphoreType.DMA((rows,)),

time: 46.8 us -> 44.1 us (0.942)
  Pallas kernels: 42.1 us -> 39.3 us
    pallas_call x1, Pallas kernels: 36.2 us -> 34.6 us  [fast_exchange(): pl.pallas_call(functools.partial(fast_kernel, sizes), out_shape=[jax.Shap...]
    pallas_call x1, Pallas kernels: 5.82 us -> 4.71 us  [fast_legendre(): pl.pallas_call(functools.partial(fast_legendre_kernel, col_count), out_sh...]
where the time goes in v3:
time: 44.1 us; the launch traced here: 43.9 us
  Pallas kernels  39.3 us (89%)
  local copies, waits for them, and re-layouts  2.57 us (6%)
  between operations  2.01 us (5%)
    pallas_call x1, Pallas kernels, fast_exchange(): pl.pallas_call(functools.partial(fast_kernel, sizes), out_shape=[jax.Shap...  34.6 us
    pallas_call x1, Pallas kernels, fast_legendre(): pl.pallas_call(functools.partial(fast_legendre_kernel, col_count), out_sh...  4.71 us
    unnamed x15, local copies, waits for them, and re-layouts  2.47 us

profile of v3, /device:TPU:0, one launch (start us, length us, event | category | flops | bytes accessed | tf_op | source)
XLA Modules:
  0.0 43.9 jit_solution(12905061775548405280)
XLA Ops:
  1.9 1.4 %copy.14 = bf16[214,640,4]{1,0,2:T(8,128)(2,1)S(1)} copy(bf16[214,640,4]{1,2,0:T(4,128)(2,1)} %param.13) | data formatting | bytes 2191360 | tf_op args[3]
  3.3 0.0 copy-start
  3.3 0.0 copy-start.1
  3.3 0.0 copy-start.2
  3.3 0.0 copy-start.3
  3.4 0.0 copy-start.4
  3.4 0.0 copy-start.5
  3.4 0.0 copy-start.6
  3.4 0.1 pad.4.weight_ref
  3.5 0.9 %copy-done = bf16[1,64,5120]{2,1,0:T(8,128)(2,1)S(1)} copy-done((bf16[1,64,5120]{2,1,0:T(8,128)(2,1)S(1)}, bf16[1,64,5120]{2,1,0:T(8,128)(2,1)}, u32[]{:S(2)}) %copy-start) | copy-done | bytes 655384
  4.4 0.2 copy-done.1
  4.5 0.0 copy-done.2
  4.5 0.0 copy-done.3
  4.6 0.0 copy-done.4
  4.6 0.0 copy-done.5
  4.6 0.0 copy-done.6
  4.6 34.6 %shard_map.113 = (bf16[8,4,224,128]{3,2,1,0:T(8,128)(2,1)S(1)}, bf16[8,112,640]{2,1,0:T(8,128)(2,1)S(1)}, f32[4,8,4096]{2,1,0:T(8,128)S(1)}) custom-call(s32[1]{0:T(128)S(6)} %copy.15.points_hbm, s32[4]{0:T(128)S(1)} %copy-done.6, s32[1]{0:T(128)S(6)} %copy.16.under_hbm, s32[856]{0:T(1024)S(1)} %copy-done.5, bf16[64,5120]{1,0:T(8,128)(2,1)S(1)} %bitcast.5, ...), custom_call_target="tpu_custom_call" | custom-call | flops 838860800 | bytes 8388608 | tf_op jit(solution)/shard_map/pallas_call | solution.py:1095
  39.2 4.7 %shard_map.114 = (f32[214,80,128]{2,1,0:T(8,128)}, f32[8,4,4096]{2,1,0:T(4,128)}) custom-call(s32[856]{0:T(1024)S(1)} %copy-done.5, bf16[8,112,640]{2,1,0:T(8,128)(2,1)S(1)} %get-tuple-element.7.weight_ref, bf16[8,4,224,128]{3,2,1,0:T(8,128)(2,1)S(1)} %get-tuple-element.8.coef_ref, f32[4,8,4096]{2,1,0:T(8,128)S(1)} %get-tuple-element.9.ocean_ref), custom_call_target="tpu_custom_call" | custom-call | flops 1174405120 | bytes 8765440 | tf_op jit(solution)/shard_map/pallas_call | solution.py:1247
Async XLA Ops:
  3.3 1.1 %copy-start = (bf16[1,64,5120]{2,1,0:T(8,128)(2,1)S(1)}, bf16[1,64,5120]{2,1,0:T(8,128)(2,1)}, u32[]{:S(2)}) copy-start(bf16[1,64,5120]{2,1,0:T(8,128)(2,1)} %param.10) | copy-start | bytes 1966084
  3.3 1.2 %copy-start.1 = (f32[8,4,4096]{2,1,0:T(4,128)S(1)}, f32[8,4,4096]{2,1,0:T(4,128)}, u32[]{:S(2)}) copy-start(f32[8,4,4096]{2,1,0:T(4,128)} %ocean_ref.1) | copy-start | bytes 1572868
  3.3 1.2 %copy-start.2 = (f32[4,4096]{1,0:T(4,128)S(1)}, f32[4,4096]{1,0:T(4,128)}, u32[]{:S(2)}) copy-start(f32[4,4096]{1,0:T(4,128)} %kappa_ref.1) | copy-start | bytes 196612
  3.3 1.2 %copy-start.3 = (f32[4,4096]{1,0:T(4,128)S(1)}, f32[4,4096]{1,0:T(4,128)}, u32[]{:S(2)}) copy-start(f32[4,4096]{1,0:T(4,128)} %depth_ref.1) | copy-start | bytes 196612
  3.4 1.2 %copy-start.4 = (s32[4,4096]{1,0:T(4,128)S(1)}, s32[4,4096]{1,0:T(4,128)}, u32[]{:S(2)}) copy-start(s32[4,4096]{1,0:T(4,128)} %water_ref.1) | copy-start | bytes 196612
  3.4 1.2 %copy-start.5 = (s32[856]{0:T(1024)S(1)}, s32[856]{0:T(1024)}, u32[]{:S(2)}) copy-start(s32[856]{0:T(1024)} %slots_hbm.3) | copy-start | bytes 10276
  3.4 1.2 %copy-start.6 = (s32[4]{0:T(128)S(1)}, s32[4]{0:T(128)}, u32[]{:S(2)}) copy-start(s32[4]{0:T(128)} %over_hbm.1) | copy-start | bytes 52

commit v4 on v3

--- a/solution.py
+++ b/solution.py
@@ -879,10 +879,6 @@
     wide = 512
     shift = span.bit_length() - 1
 
-    def halves_of(value):
-        upper = value.astype(jnp.bfloat16).astype(jnp.float32)
-        return upper, value - upper
-
     def columns_of(start):
         place = start + lax.broadcasted_iota(jnp.int32, (1, wide), 1)
         return lax.shift_right_logical(place * points, shift)
@@ -906,13 +902,13 @@
     meridional = x_ref[strata + bottom : strata + bottom + 1].astype(jnp.float32)
     air = x_ref[2 * strata + bottom : 2 * strata + bottom + 1].astype(jnp.float32)
     speed = thermal_transfer_factor * jnp.sqrt(zonal * zonal + meridional * meridional + 1.0)
-    table = table_of([*halves_of(speed), air])
+    table = table_of([speed, air])
 
     @pl.loop(0, span // wide)
     def _(k):
         start = pl.multiple_of(k * wide, wide)
-        upper, lower, below = pick(table, columns_of(start))
-        local_ref[0:1, pl.ds(start, wide)] = upper + lower
+        brisk, below = pick(table, columns_of(start))
+        local_ref[0:1, pl.ds(start, wide)] = brisk
         local_ref[1:2, pl.ds(start, wide)] = below
 
     @pl.when(has_next)
@@ -946,7 +942,7 @@
     skin = jnp.zeros((1, span), jnp.float32)
     for r in range(3 * rows):
         skin = jnp.where(under == r, heat_ref[0, r, 0:1, :], skin)
-    skin_table = table_of(halves_of(skin))
+    skin_table = table_of([skin])
     inverse = 1.0 / jnp.full((1, wide), points, jnp.int32).astype(jnp.float32)
 
     @pl.loop(0, span // wide)
@@ -957,9 +953,9 @@
         rest = scaled - index * points
         index = jnp.where(rest < 0, index - 1, jnp.where(rest >= points, index + 1, index))
         index = jnp.minimum(index, span - 1)
-        upper, lower = pick(skin_table, index)
+        (mapped,) = pick(skin_table, index)
         cut = pl.ds(start, wide)
-        flux_ref[len(REACH), 0:1, cut] = local_ref[0:1, cut] * (upper + lower - local_ref[1:2, cut])
+        flux_ref[len(REACH), 0:1, cut] = local_ref[0:1, cut] * (mapped - local_ref[1:2, cut])
 
     lane = lax.broadcasted_iota(jnp.int32, (1, 128), 1)
     relative = jnp.zeros((1, 128), jnp.float32)
@@ -1023,11 +1019,7 @@
             else:
                 thermal_out[r - rows] = fresh
 
-    ocean_step(0)
-    ocean_step(1)
-
-    @pl.loop(0, lat_count)
-    def _(step):
+    def forward(step):
         line_row = (lat + lat_count - step) % lat_count
         direct_copy(0, line_row).wait_recv()
 
@@ -1043,6 +1035,13 @@
             diag_copy(1, line_row).start()
 
         chip_copy(2, line_row).start()
+
+    ocean_step(0)
+    forward(0)
+    forward(1)
+    ocean_step(1)
+    forward(2)
+    forward(3)
 
     ocean_step(2)
     ocean_step(3)

time: 44.1 us -> 43.2 us (0.980)
  Pallas kernels: 39.3 us -> 38.4 us
    pallas_call x1, Pallas kernels: 34.6 us -> 33.7 us  [fast_exchange(): pl.pallas_call(functools.partial(fast_kernel, sizes), out_shape=[jax.Shap...]
where the time goes in v4:
time: 43.2 us; the launch traced here: 43 us
  Pallas kernels  38.4 us (89%)
  local copies, waits for them, and re-layouts  2.57 us (6%)
  between operations  2.01 us (5%)
    pallas_call x1, Pallas kernels, fast_exchange(): pl.pallas_call(functools.partial(fast_kernel, sizes), out_shape=[jax.Shap...  33.7 us
    pallas_call x1, Pallas kernels, fast_legendre(): pl.pallas_call(functools.partial(fast_legendre_kernel, col_count), out_sh...  4.71 us
    unnamed x15, local copies, waits for them, and re-layouts  2.47 us

profile of v4, /device:TPU:0, one launch (start us, length us, event | category | flops | bytes accessed | tf_op | source)
XLA Modules:
  0.0 43.0 jit_solution(3649818651756248843)
XLA Ops:
  1.9 1.4 %copy.14 = bf16[214,640,4]{1,0,2:T(8,128)(2,1)S(1)} copy(bf16[214,640,4]{1,2,0:T(4,128)(2,1)} %param.13) | data formatting | bytes 2191360 | tf_op args[3]
  3.3 0.0 copy-start
  3.3 0.0 copy-start.1
  3.3 0.0 copy-start.2
  3.3 0.0 copy-start.3
  3.4 0.0 copy-start.4
  3.4 0.0 copy-start.5
  3.4 0.0 copy-start.6
  3.4 0.1 pad.4.weight_ref
  3.5 0.9 %copy-done = bf16[1,64,5120]{2,1,0:T(8,128)(2,1)S(1)} copy-done((bf16[1,64,5120]{2,1,0:T(8,128)(2,1)S(1)}, bf16[1,64,5120]{2,1,0:T(8,128)(2,1)}, u32[]{:S(2)}) %copy-start) | copy-done | bytes 655384
  4.4 0.2 copy-done.1
  4.5 0.0 copy-done.2
  4.5 0.0 copy-done.3
  4.6 0.0 copy-done.4
  4.6 0.0 copy-done.5
  4.6 0.0 copy-done.6
  4.6 33.7 %shard_map.113 = (bf16[8,4,224,128]{3,2,1,0:T(8,128)(2,1)S(1)}, bf16[8,112,640]{2,1,0:T(8,128)(2,1)S(1)}, f32[4,8,4096]{2,1,0:T(8,128)S(1)}) custom-call(s32[1]{0:T(128)S(6)} %copy.15.points_hbm, s32[4]{0:T(128)S(1)} %copy-done.6, s32[1]{0:T(128)S(6)} %copy.16.under_hbm, s32[856]{0:T(1024)S(1)} %copy-done.5, bf16[64,5120]{1,0:T(8,128)(2,1)S(1)} %bitcast.5, ...), custom_call_target="tpu_custom_call" | custom-call | flops 838860800 | bytes 8388608 | tf_op jit(solution)/shard_map/pallas_call | solution.py:1094
  38.2 4.7 %shard_map.114 = (f32[214,80,128]{2,1,0:T(8,128)}, f32[8,4,4096]{2,1,0:T(4,128)}) custom-call(s32[856]{0:T(1024)S(1)} %copy-done.5, bf16[8,112,640]{2,1,0:T(8,128)(2,1)S(1)} %get-tuple-element.7.weight_ref, bf16[8,4,224,128]{3,2,1,0:T(8,128)(2,1)S(1)} %get-tuple-element.8.coef_ref, f32[4,8,4096]{2,1,0:T(8,128)S(1)} %get-tuple-element.9.ocean_ref), custom_call_target="tpu_custom_call" | custom-call | flops 1174405120 | bytes 8765440 | tf_op jit(solution)/shard_map/pallas_call | solution.py:1246
Async XLA Ops:
  3.3 1.1 %copy-start = (bf16[1,64,5120]{2,1,0:T(8,128)(2,1)S(1)}, bf16[1,64,5120]{2,1,0:T(8,128)(2,1)}, u32[]{:S(2)}) copy-start(bf16[1,64,5120]{2,1,0:T(8,128)(2,1)} %param.10) | copy-start | bytes 1966084
  3.3 1.2 %copy-start.1 = (f32[8,4,4096]{2,1,0:T(4,128)S(1)}, f32[8,4,4096]{2,1,0:T(4,128)}, u32[]{:S(2)}) copy-start(f32[8,4,4096]{2,1,0:T(4,128)} %ocean_ref.1) | copy-start | bytes 1572868
  3.3 1.2 %copy-start.2 = (f32[4,4096]{1,0:T(4,128)S(1)}, f32[4,4096]{1,0:T(4,128)}, u32[]{:S(2)}) copy-start(f32[4,4096]{1,0:T(4,128)} %kappa_ref.1) | copy-start | bytes 196612
  3.3 1.2 %copy-start.3 = (f32[4,4096]{1,0:T(4,128)S(1)}, f32[4,4096]{1,0:T(4,128)}, u32[]{:S(2)}) copy-start(f32[4,4096]{1,0:T(4,128)} %depth_ref.1) | copy-start | bytes 196612
  3.4 1.2 %copy-start.4 = (s32[4,4096]{1,0:T(4,128)S(1)}, s32[4,4096]{1,0:T(4,128)}, u32[]{:S(2)}) copy-start(s32[4,4096]{1,0:T(4,128)} %water_ref.1) | copy-start | bytes 196612
  3.4 1.2 %copy-start.5 = (s32[856]{0:T(1024)S(1)}, s32[856]{0:T(1024)}, u32[]{:S(2)}) copy-start(s32[856]{0:T(1024)} %slots_hbm.3) | copy-start | bytes 10276
  3.4 1.2 %copy-start.6 = (s32[4]{0:T(128)S(1)}, s32[4]{0:T(128)}, u32[]{:S(2)}) copy-start(s32[4]{0:T(128)} %over_hbm.1) | copy-start | bytes 52

commit v5 on v4

--- a/solution.py
+++ b/solution.py
@@ -1215,16 +1215,17 @@
             both = jnp.concatenate(
                 [jnp.where(odd, nothing, coefs), jnp.where(odd, coefs, nothing)], axis=1
             )
-            left = jnp.concatenate(
-                [jnp.where(lane_pair == j, values, jnp.zeros_like(values)) for j in range(8)], axis=0
-            )
-            summed = jnp.dot(left, both, preferred_element_type=jnp.float32)
-            for s in range(16):
-                wave = slots_ref[jnp.minimum(first_slot + block * 16 + s, last_slot)]
-                part = summed[
-                    s // 2 * degrees : (s // 2 + 1) * degrees, s % 2 * width : (s % 2 + 1) * width
-                ]
-                made_ref[block * 16 + s] = jnp.where(degree >= wave, part, 0.0)
+            for q in range(0, 8, 4):
+                left = jnp.concatenate(
+                    [jnp.where(lane_pair == j, values, jnp.zeros_like(values)) for j in range(q, q + 4)],
+                    axis=0,
+                )
+                summed = jnp.dot(left, both, preferred_element_type=jnp.float32)
+                for s in range(2 * q, 2 * q + 8):
+                    wave = slots_ref[jnp.minimum(first_slot + block * 16 + s, last_slot)]
+                    low = (s // 2 - q) * degrees
+                    part = summed[low : low + degrees, s % 2 * width : (s % 2 + 1) * width]
+                    made_ref[block * 16 + s] = jnp.where(degree >= wave, part, 0.0)
 
             made_copy(block, 16 if block < blocks - 1 else rest).start()
 

time: 43.2 us -> 43 us (level)
  no operation moved by 1% of the time
where the time goes in v5:
time: 43 us; the launch traced here: 42.8 us
  Pallas kernels  38.2 us (89%)
  local copies, waits for them, and re-layouts  2.57 us (6%)
  between operations  2.01 us (5%)
    pallas_call x1, Pallas kernels, fast_exchange(): pl.pallas_call(functools.partial(fast_kernel, sizes), out_shape=[jax.Shap...  33.7 us
    pallas_call x1, Pallas kernels, fast_legendre(): pl.pallas_call(functools.partial(fast_legendre_kernel, col_count), out_sh...  4.52 us
    unnamed x15, local copies, waits for them, and re-layouts  2.47 us

profile of v5, /device:TPU:0, one launch (start us, length us, event | category | flops | bytes accessed | tf_op | source)
XLA Modules:
  0.0 42.8 jit_solution(10064047251192558636)
XLA Ops:
  1.9 1.4 %copy.14 = bf16[214,640,4]{1,0,2:T(8,128)(2,1)S(1)} copy(bf16[214,640,4]{1,2,0:T(4,128)(2,1)} %param.13) | data formatting | bytes 2191360 | tf_op args[3]
  3.3 0.0 copy-start
  3.3 0.0 copy-start.1
  3.3 0.0 copy-start.2
  3.3 0.0 copy-start.3
  3.4 0.0 copy-start.4
  3.4 0.0 copy-start.5
  3.4 0.0 copy-start.6
  3.4 0.1 pad.4.weight_ref
  3.5 0.9 %copy-done = bf16[1,64,5120]{2,1,0:T(8,128)(2,1)S(1)} copy-done((bf16[1,64,5120]{2,1,0:T(8,128)(2,1)S(1)}, bf16[1,64,5120]{2,1,0:T(8,128)(2,1)}, u32[]{:S(2)}) %copy-start) | copy-done | bytes 655384
  4.4 0.2 copy-done.1
  4.5 0.0 copy-done.2
  4.5 0.0 copy-done.3
  4.6 0.0 copy-done.4
  4.6 0.0 copy-done.5
  4.6 0.0 copy-done.6
  4.6 33.7 %shard_map.113 = (bf16[8,4,224,128]{3,2,1,0:T(8,128)(2,1)S(1)}, bf16[8,112,640]{2,1,0:T(8,128)(2,1)S(1)}, f32[4,8,4096]{2,1,0:T(8,128)S(1)}) custom-call(s32[1]{0:T(128)S(6)} %copy.15.points_hbm, s32[4]{0:T(128)S(1)} %copy-done.6, s32[1]{0:T(128)S(6)} %copy.16.under_hbm, s32[856]{0:T(1024)S(1)} %copy-done.5, bf16[64,5120]{1,0:T(8,128)(2,1)S(1)} %bitcast.5, ...), custom_call_target="tpu_custom_call" | custom-call | flops 838860800 | bytes 8388608 | tf_op jit(solution)/shard_map/pallas_call | solution.py:1094
  38.2 4.5 %shard_map.114 = (f32[214,80,128]{2,1,0:T(8,128)}, f32[8,4,4096]{2,1,0:T(4,128)}) custom-call(s32[856]{0:T(1024)S(1)} %copy-done.5, bf16[8,112,640]{2,1,0:T(8,128)(2,1)S(1)} %get-tuple-element.7.weight_ref, bf16[8,4,224,128]{3,2,1,0:T(8,128)(2,1)S(1)} %get-tuple-element.8.coef_ref, f32[4,8,4096]{2,1,0:T(8,128)S(1)} %get-tuple-element.9.ocean_ref), custom_call_target="tpu_custom_call" | custom-call | flops 1174405120 | bytes 8765440 | tf_op jit(solution)/shard_map/pallas_call | solution.py:1247
Async XLA Ops:
  3.3 1.1 %copy-start = (bf16[1,64,5120]{2,1,0:T(8,128)(2,1)S(1)}, bf16[1,64,5120]{2,1,0:T(8,128)(2,1)}, u32[]{:S(2)}) copy-start(bf16[1,64,5120]{2,1,0:T(8,128)(2,1)} %param.10) | copy-start | bytes 1966084
  3.3 1.2 %copy-start.1 = (f32[8,4,4096]{2,1,0:T(4,128)S(1)}, f32[8,4,4096]{2,1,0:T(4,128)}, u32[]{:S(2)}) copy-start(f32[8,4,4096]{2,1,0:T(4,128)} %ocean_ref.1) | copy-start | bytes 1572868
  3.3 1.2 %copy-start.2 = (f32[4,4096]{1,0:T(4,128)S(1)}, f32[4,4096]{1,0:T(4,128)}, u32[]{:S(2)}) copy-start(f32[4,4096]{1,0:T(4,128)} %kappa_ref.1) | copy-start | bytes 196612
  3.3 1.2 %copy-start.3 = (f32[4,4096]{1,0:T(4,128)S(1)}, f32[4,4096]{1,0:T(4,128)}, u32[]{:S(2)}) copy-start(f32[4,4096]{1,0:T(4,128)} %depth_ref.1) | copy-start | bytes 196612
  3.4 1.2 %copy-start.4 = (s32[4,4096]{1,0:T(4,128)S(1)}, s32[4,4096]{1,0:T(4,128)}, u32[]{:S(2)}) copy-start(s32[4,4096]{1,0:T(4,128)} %water_ref.1) | copy-start | bytes 196612
  3.4 1.2 %copy-start.5 = (s32[856]{0:T(1024)S(1)}, s32[856]{0:T(1024)}, u32[]{:S(2)}) copy-start(s32[856]{0:T(1024)} %slots_hbm.3) | copy-start | bytes 10276
  3.4 1.2 %copy-start.6 = (s32[4]{0:T(128)S(1)}, s32[4]{0:T(128)}, u32[]{:S(2)}) copy-start(s32[4]{0:T(128)} %over_hbm.1) | copy-start | bytes 52
